TPU v7x, 256 devices: a whole 4x4x8 slice. The times are simulated.
256 devices in a mesh: rows: 32 (over z_hi, y, core), sub: 8 (over x, z_lo).
Axes of the slice: x: 4, y: 4, z: 8 (z_hi: 4, z_lo: 2; z = z_hi * 2 + z_lo), core: 2. Of those that a mesh axis runs over, the one named last changes fastest.
Arguments:
- features: bfloat16 [1048576, 512], P(('rows', 'sub')), may hold values from -16 to 16
- residual: float32 [1048576, 128], P(('rows', 'sub')), may hold values from -6 to 6
- coefficients: float32 [1048576, 128], P(('rows', 'sub')), may hold values from -6 to 6
- block_owner: int32 [2], replicated, may hold values from 0 to 255
- block_tiles: int32 [2, 4], replicated, may hold values from 0 to 31, as said below
Outputs:
- residual_out: float32 [1048576, 128], P(('rows', 'sub'))
- coefficients_out: float32 [1048576, 128], P(('rows', 'sub'))
Inputs may be any that keep to these rules, and one draw needn't show every extreme that they name: `block_tiles`: in each step the tile numbers are distinct, and tiles 0 and 31 are among them.
All inputs are finite; a program needn't handle non-finite values.
Results may differ from a plain program's by a relative error of at most 0.0012.
Values may be sent and summed in bfloat16 or wider, within the bound.
A program may use at most 128 MiB of HBM per device.

v0:
```python
import math

import jax
import jax.numpy as jnp
from jax import lax
from jax.sharding import PartitionSpec as P

BLOCK = 512
TILE = 128
STEPS = 2


RIDGE = 0.5


def from_root(value, axis, source):
    kept = jnp.where(lax.axis_index(axis) == source, value, 0).astype(value.dtype)
    return lax.psum(kept, axis)


def kernel_slab(left_rows, right_rows, left_norm, right_norm, kernel_scale):
    cross_dot = jnp.einsum("rf,bf->rb", left_rows, right_rows, preferred_element_type=jnp.float32)
    distance = left_norm[:, None] + right_norm[None, :] - 2.0 * cross_dot
    return jnp.exp(-kernel_scale * distance)


def block_solve(kernel_bb, gradient):
    size_now = kernel_bb.shape[0]
    system = kernel_bb + RIDGE * jnp.eye(size_now, dtype=jnp.float32)
    factor = jnp.linalg.cholesky(system)
    half_way = lax.linalg.triangular_solve(factor, gradient, left_side=True, lower=True)
    return lax.linalg.triangular_solve(
        factor, half_way, left_side=True, lower=True, transpose_a=True
    )


def fetch_block(features, owner_now, tile_ids):
    rows_dev, width = features.shape
    picked = features.reshape(rows_dev // TILE, TILE, width)[tile_ids].reshape(BLOCK, width)
    return from_root(picked, ("rows", "sub"), owner_now)


def local(features, residual, coefficients, block_owner, block_tiles):
    rows_dev, width = features.shape
    targets = residual.shape[1]
    sub_count = lax.axis_size("sub")
    devices = lax.axis_size("rows") * sub_count
    self_index = lax.axis_index("rows") * sub_count + lax.axis_index("sub")
    kernel_scale = 1.0 / width
    step_size = 1.0 / math.sqrt(rows_dev * devices)
    row_norms = jnp.einsum("rf,rf->r", features, features, preferred_element_type=jnp.float32)
    for step_index in range(STEPS):
        owner_now = block_owner[step_index]
        tile_ids = block_tiles[step_index]
        block_rows = fetch_block(features, owner_now, tile_ids)
        block_norm = jnp.einsum(
            "bf,bf->b", block_rows, block_rows, preferred_element_type=jnp.float32
        )
        slab = kernel_slab(features, block_rows, row_norms, block_norm, kernel_scale).astype(
            jnp.bfloat16
        )
        weighted = (residual - RIDGE * coefficients).astype(jnp.bfloat16)
        local_term = jnp.einsum("rb,rc->bc", slab, weighted, preferred_element_type=jnp.float32)
        gradient = lax.psum(local_term, ("rows", "sub"))
        kernel_bb = kernel_slab(block_rows, block_rows, block_norm, block_norm, kernel_scale)
        update = block_solve(kernel_bb, gradient) * step_size
        update_low = update.astype(jnp.bfloat16)
        residual = residual - jnp.dot(slab, update_low, preferred_element_type=jnp.float32)
        contribution = jnp.where(self_index == owner_now, update, jnp.zeros_like(update))
        tiled = coefficients.reshape(rows_dev // TILE, TILE, targets)
        tiled = tiled.at[tile_ids].add(contribution.reshape(BLOCK // TILE, TILE, targets))
        coefficients = tiled.reshape(rows_dev, targets)
    return (residual, coefficients)


def solution(mesh):
    in_specs = (
        P(("rows", "sub"), None),
        P(("rows", "sub"), None),
        P(("rows", "sub"), None),
        P(),
        P(),
    )
    out_specs = (P(("rows", "sub"), None), P(("rows", "sub"), None))
    return jax.shard_map(local, mesh=mesh, in_specs=in_specs, out_specs=out_specs, check_vma=False)
```

profile of v0, /device:TPU:1, one launch (start us, length us, event | category | flops | bytes accessed | tf_op | source)
XLA Modules:
  0.0 927.1 jit_solution(9409309612680811841)
XLA Ops:
  7.2 1.6 copy.60
  9.4 2.8 gather_fusion
  12.2 2.8 gather_fusion.1
  18.0 3.1 fusion.6
  21.1 255.5 %all-reduce.10.cloned.1.call-done = (bf16[512,512]{1,0:T(8,128)(2,1)}, bf16[512,512]{1,0:T(8,128)(2,1)}) async-done(((bf16[512,512]{1,0:T(8,128)(2,1)}, bf16[512,512]{1,0:T(8,128)(2,1)}), (bf16[512,512]{1,0:T(8,128)(2,1)}, bf16[512,512]{1,0:T(8,128)(2,1)})) %all-reduce.10.cloned.1.call-update) | async-done | bytes 1048592 | tf_op jit(solution)/shard_map/psum | solution.py:18
  276.6 1.2 fusion.18
  277.8 1.8 select_add_fusion.1
  279.6 7.0 fusion.5
  286.7 4.6 fusion.2
  291.3 1.5 select_add_fusion
  292.8 1.3 copy.8
  294.1 1.4 fusion.17
  296.6 11.7 %cholesky.286 = f32[128,128]{1,0:T(8,128)S(1)} custom-call(f32[128,128]{1,0:T(8,128)S(1)} %cholesky.426), custom_call_target="Cholesky" | custom-call | tf_op jit(solution)/shard_map/jit(cholesky)/cholesky | solution.py:30
  308.4 10.0 %custom-call.31 = f32[1,128,128]{1,2,0:T(8,128)S(1)} custom-call(f32[1,128,128]{2,1,0:T(8,128)S(1)} %get-tuple-element.78), custom_call_target="InvertDiagBlocksLowerTriangular" | custom-call | tf_op jit(solution)/shard_map/jit(cholesky)/cholesky | solution.py:30
  318.4 1.2 constant_dynamic-update-slice_fusion.5
  319.6 1.3 convolution_subtract_fusion.3
  320.9 11.7 %cholesky.305 = f32[128,128]{1,0:T(8,128)S(1)} custom-call(f32[128,128]{1,0:T(8,128)S(1)} %cholesky.430), custom_call_target="Cholesky" | custom-call | tf_op jit(solution)/shard_map/jit(cholesky)/cholesky | solution.py:30
  332.7 9.8 %custom-call.32 = f32[1,128,128]{1,2,0:T(8,128)S(1)} custom-call(f32[1,128,128]{2,1,0:T(8,128)S(1)} %get-tuple-element.75), custom_call_target="InvertDiagBlocksLowerTriangular" | custom-call | tf_op jit(solution)/shard_map/jit(cholesky)/cholesky | solution.py:30
  342.8 1.3 convolution_subtract_fusion.5
  344.1 11.9 %cholesky.326 = f32[128,128]{1,0:T(8,128)S(1)} custom-call(f32[128,128]{1,0:T(8,128)S(1)} %cholesky.435), custom_call_target="Cholesky" | custom-call | tf_op jit(solution)/shard_map/jit(cholesky)/cholesky | solution.py:30
  356.0 9.8 %custom-call.33 = f32[1,128,128]{1,2,0:T(8,128)S(1)} custom-call(f32[1,128,128]{2,1,0:T(8,128)S(1)} %get-tuple-element.72), custom_call_target="InvertDiagBlocksLowerTriangular" | custom-call | tf_op jit(solution)/shard_map/jit(cholesky)/cholesky | solution.py:30
  366.0 1.2 convolution_subtract_fusion.19
  367.3 11.7 %cholesky.343 = f32[128,128]{1,0:T(8,128)S(1)} custom-call(f32[128,128]{1,0:T(8,128)S(1)} %convolution_subtract_fusion.19), custom_call_target="Cholesky" | custom-call | tf_op jit(solution)/shard_map/jit(cholesky)/cholesky | solution.py:30
  381.6 4.8 fusion.14
  390.9 14.5 %while.8 = (s32[]{:T(128)}, f32[512,512]{1,0:T(8,128)}, s32[4,2]{0,1:T(2,128)S(1)}, f32[4,128,128]{2,1,0:T(8,128)}, s32[]{:T(128)}) while((s32[]{:T(128)}, f32[512,512]{1,0:T(8,128)}, s32[4,2]{0,1:T(2,128)S(1)}, f32[4,128,128]{2,1,0:T(8,128)}, s32[]{:T(128)}) %tuple.66), condition=%wide.while_cond.1, body=%wide.while_body.1.sunk | while | flops 2 | bytes 132205 | solution.py:32
  391.5 2.9 bitcast_dynamic-update-slice_fusion.4
  395.1 2.9 bitcast_dynamic-update-slice_fusion.4
  398.6 2.9 bitcast_dynamic-update-slice_fusion.4
  402.2 2.8 bitcast_dynamic-update-slice_fusion.4
  405.4 1.6 copy.10
  407.0 1.5 fusion.15
  409.4 11.7 %cholesky.358 = f32[128,128]{1,0:T(8,128)S(1)} custom-call(f32[128,128]{1,0:T(8,128)S(1)} %cholesky.439), custom_call_target="Cholesky" | custom-call | tf_op jit(solution)/shard_map/jit(cholesky)/cholesky | solution.py:30
  421.3 9.8 %custom-call.36 = f32[1,128,128]{1,2,0:T(8,128)S(1)} custom-call(f32[1,128,128]{2,1,0:T(8,128)S(1)} %get-tuple-element.68), custom_call_target="InvertDiagBlocksLowerTriangular" | custom-call | tf_op jit(solution)/shard_map/jit(cholesky)/cholesky | solution.py:30
  431.1 1.2 constant_dynamic-update-slice_fusion.3
  432.3 1.3 convolution_subtract_fusion.2
  433.6 11.7 %cholesky.377 = f32[128,128]{1,0:T(8,128)S(1)} custom-call(f32[128,128]{1,0:T(8,128)S(1)} %cholesky.443), custom_call_target="Cholesky" | custom-call | tf_op jit(solution)/shard_map/jit(cholesky)/cholesky | solution.py:30
  445.4 10.0 %custom-call.37 = f32[1,128,128]{1,2,0:T(8,128)S(1)} custom-call(f32[1,128,128]{2,1,0:T(8,128)S(1)} %get-tuple-element.65), custom_call_target="InvertDiagBlocksLowerTriangular" | custom-call | tf_op jit(solution)/shard_map/jit(cholesky)/cholesky | solution.py:30
  455.6 1.3 convolution_subtract_fusion.4
  456.9 11.7 %cholesky.398 = f32[128,128]{1,0:T(8,128)S(1)} custom-call(f32[128,128]{1,0:T(8,128)S(1)} %cholesky.448), custom_call_target="Cholesky" | custom-call | tf_op jit(solution)/shard_map/jit(cholesky)/cholesky | solution.py:30
  468.6 9.8 %custom-call.38 = f32[1,128,128]{1,2,0:T(8,128)S(1)} custom-call(f32[1,128,128]{2,1,0:T(8,128)S(1)} %get-tuple-element.62), custom_call_target="InvertDiagBlocksLowerTriangular" | custom-call | tf_op jit(solution)/shard_map/jit(cholesky)/cholesky | solution.py:30
  478.7 1.2 convolution_subtract_fusion.16
  479.9 11.7 %cholesky.415 = f32[128,128]{1,0:T(8,128)S(1)} custom-call(f32[128,128]{1,0:T(8,128)S(1)} %convolution_subtract_fusion.16), custom_call_target="Cholesky" | custom-call | tf_op jit(solution)/shard_map/jit(cholesky)/cholesky | solution.py:30
  496.8 1.3 select_select_fusion
  498.1 40.1 %custom-call.35 = f32[4,128,128]{1,2,0:T(8,128)S(1)} custom-call(f32[4,128,128]{2,1,0:T(8,128)} %get-tuple-element.34), custom_call_target="InvertDiagBlocksLowerTriangular" | custom-call | tf_op jit(solution)/shard_map/triangular_solve/custom-call.8 | solution.py:32
  538.3 98.6 %all-reduce.6.cloned.1.call-done = f32[512,128]{1,0:T(8,128)} async-done(((f32[512,128]{1,0:T(8,128)}), f32[512,128]{1,0:T(8,128)}) %all-reduce.6.cloned.1.call-update) | async-done | bytes 262160 | tf_op jit(solution)/shard_map/psum | solution.py:64
  639.3 1.2 convolution_subtract_fusion.12
  640.8 1.3 convolution_subtract_fusion.18
  642.6 1.1 convolution_subtract_fusion.11
  643.9 1.3 convolution_subtract_fusion.10
  645.4 1.4 convolution_subtract_fusion.17
  648.1 2.0 copy-done
  650.1 4.6 fusion.7
  654.7 1.9 fusion.130
  656.7 7.6 while.9
  657.3 1.3 bitcast_dynamic-update-slice_fusion.5
  659.2 1.3 bitcast_dynamic-update-slice_fusion.5
  661.1 1.3 bitcast_dynamic-update-slice_fusion.5
  663.0 1.3 bitcast_dynamic-update-slice_fusion.5
  665.0 40.4 %custom-call.40 = f32[4,128,128]{1,2,0:T(8,128)S(1)} custom-call(f32[4,128,128]{2,1,0:T(8,128)} %copy-done.9), custom_call_target="InvertDiagBlocksLowerTriangular" | custom-call | tf_op jit(solution)/shard_map/triangular_solve/custom-call.8 | solution.py:32
  705.4 200.9 %all-reduce.8.cloned.1.call-done = f32[512,128]{1,0:T(8,128)} async-done(((f32[512,128]{1,0:T(8,128)}), f32[512,128]{1,0:T(8,128)}) %all-reduce.8.cloned.1.call-update) | async-done | bytes 262160 | tf_op jit(solution)/shard_map/psum | solution.py:64
  906.3 1.3 fusion.82
  910.3 1.2 convolution_subtract_fusion.15
  913.8 4.3 convolution_subtract_fusion
  918.9 1.3 copy-done.3
  (109 shorter events, 29.5 us)
Async XLA Ops:
  7.2 1.7 copy-start.10
  7.2 1.7 copy-start.11
  7.2 269.4 %all-reduce.10.cloned.1.call-start = ((), (), s32[]{:S(2)}) async-start(), calls=%async_computation.2 | async-start | bytes 2097152 | tf_op jit(solution)/shard_map/psum | solution.py:18
  18.0 618.9 %all-reduce.6.cloned.1.call-start = ((), (), s32[]{:S(2)}) async-start(), calls=%async_computation | async-start | bytes 524288 | tf_op jit(solution)/shard_map/psum | solution.py:64
  279.6 7.0 copy-start.8
  279.6 7.2 copy-start.4
  295.6 1.0 copy-start.6
  386.5 519.8 %all-reduce.8.cloned.1.call-start = ((), (), s32[]{:S(2)}) async-start(), calls=%async_computation.1 | async-start | bytes 524288 | tf_op jit(solution)/shard_map/psum | solution.py:64
  408.4 1.0 copy-start.7
  647.9 2.2 copy-start
  650.1 4.6 copy-start.1
  654.7 2.0 copy-start.5
  664.3 0.7 copy-start.9
  906.3 7.6 copy-start.2
  918.9 1.3 copy-start.3
Sparse Core Ops, SparseCore 0:
  18.1 258.4 all-reduce.9
  386.6 250.1 all-reduce.5
  656.8 249.4 all-reduce.7
where the time goes:
time: 938 us; the launch traced here: 927 us
  waiting for transfers between devices  555 us (59%)
  other arithmetic  252 us (27%)
  matrix products  58.9 us (6%)
  local copies, waits for them, and re-layouts  39.3 us (4%)
  between operations  21.1 us (2%)
    psum x2, waiting for transfers between devices, local(): gradient = lax.psum(local_term, ('rows', 'sub'))  299 us
    psum x1, waiting for transfers between devices, from_root(): return lax.psum(kept, axis)  255 us
    another operation x30, other arithmetic, block_solve(): factor = jnp.linalg.cholesky(system)  159 us
    another operation x5, other arithmetic, block_solve(): lax.linalg.triangular_solve(factor, half_way, left_side=True, lower=True,...  82.9 us
    another operation x27, local copies, waits for them, and re-layouts, block_solve(): lax.linalg.triangular_solve(factor, half_way, left_side=True, lower=True,...  22.4 us
  transfers between devices with their start and end apart: 3, of which 3 were waited for; matrix products, arithmetic and copies ran while one was open for 21% of the time, Pallas kernels for 0%

commit v1 on v0

v1 whole, which is shorter than its diff:
```python
import functools
import math

import jax
import jax.numpy as jnp
from jax import lax
from jax.experimental import pallas as pl
from jax.experimental.pallas import tpu as pltpu
from jax.sharding import PartitionSpec as P

MESH = pl.DeviceIdType.MESH
HI = lax.Precision.HIGHEST
F32 = jnp.float32
BF16 = jnp.bfloat16

BLOCK = 512
TILE = 128
STEPS = 2
RIDGE = 0.5
WIDTH = 512
TARGETS = 128
NX, NY, NZ = 4, 4, 8
NQ = NX * NY
CHUNK = 512
VMEM_BYTES = 56 << 20


def vmem():
    return pl.BlockSpec(memory_space=pltpu.VMEM)


def smem():
    return pl.BlockSpec(memory_space=pltpu.SMEM)


def dot(a, b, precision=None):
    return jnp.dot(a, b, precision=precision, preferred_element_type=F32)


def dot_nt(a, b, precision=None):
    return lax.dot_general(
        a, b, (((1,), (1,)), ((), ())), precision=precision, preferred_element_type=F32
    )


def place():
    across, within = lax.axis_index("rows"), lax.axis_index("sub")
    core = lax.rem(across, 2)
    y = lax.rem(lax.div(across, 2), NY)
    z = lax.div(across, 2 * NY) * 2 + lax.rem(within, 2)
    x = lax.div(within, 2)
    return x * NY + y, z, core


def device(q, z, core):
    x, y = lax.div(q, NY), lax.rem(q, NY)
    return (lax.div(z, 2) * (2 * NY) + y * 2 + core, x * 2 + lax.rem(z, 2))


def ring(start, step, size):
    return lax.rem(start + step, size)


def greet(q, z, core):
    barrier = pltpu.get_barrier_semaphore()
    pl.semaphore_signal(barrier, inc=1, device_id=device(q, z, 1 - core), device_id_type=MESH)

    @pl.loop(1, NQ)
    def _(i):
        pl.semaphore_signal(
            barrier, inc=1, device_id=device(ring(q, i, NQ), z, core), device_id_type=MESH
        )

    @pl.loop(1, NZ)
    def _(i):
        pl.semaphore_signal(
            barrier, inc=1, device_id=device(q, ring(z, i, NZ), core), device_id_type=MESH
        )

    pl.semaphore_wait(barrier, 1 + (NQ - 1) + (NZ - 1))


def remote(source, target, send_sem, recv_sem, where):
    return pltpu.make_async_remote_copy(
        src_ref=source,
        dst_ref=target,
        send_sem=send_sem,
        recv_sem=recv_sem,
        device_id=where,
        device_id_type=MESH,
    )


STAGE_SEMS = [
    pltpu.SemaphoreType.DMA((2, NQ)),
    pltpu.SemaphoreType.DMA((2, NQ)),
    pltpu.SemaphoreType.DMA((2, 2, NZ)),
    pltpu.SemaphoreType.DMA((2, 2, NZ)),
    pltpu.SemaphoreType.DMA((2, NQ)),
    pltpu.SemaphoreType.DMA((2, NQ)),
]


class Sum:
    def __init__(self, part, total, recv_a, half, recv_b, cut, recv_c, joined, sems, spot):
        self.part, self.total, self.recv_a, self.half = part, total, recv_a, half
        self.recv_b, self.cut, self.recv_c, self.joined = recv_b, cut, recv_c, joined
        self.sems = sems
        self.q, self.z, self.core = spot
        self.rows, self.lanes = half.shape[1], half.shape[2]
        self.high = cut.shape[1]
        self.tiles = cut.shape[0]
        self.rounds = 2 if self.tiles > NZ else 1

    def a_copy(self, i):
        q, z, core = self.q, self.z, self.core
        at = ring(q, i, NQ)
        sem = self.sems[0]
        return remote(
            self.part.at[1 - core, at],
            self.recv_a.at[at],
            sem.at[0, at],
            sem.at[1, at],
            device(q, z, 1 - core),
        )

    def start_a(self):
        @pl.loop(1, NQ + 1)
        def _(i):
            self.a_copy(i).start()

    def b_copy(self, i, arriving):
        q, z, core = self.q, self.z, self.core
        there = ring(q, i, NQ)
        sem = self.sems[1]
        slot = there if arriving else q
        return remote(
            self.half.at[there],
            self.recv_b.at[slot],
            sem.at[0, there],
            sem.at[1, slot],
            device(there, z, core),
        )

    def a_to_b(self):
        @pl.loop(1, NQ + 1)
        def _(i):
            at = ring(self.q, i, NQ)
            self.a_copy(i).wait_recv()
            self.half[at] = self.part[self.core, at] + self.recv_a[at]

            @pl.when(i < NQ)
            def _():
                self.b_copy(i, False).start()

    def tile_of(self, z, turn):
        return z if turn == 0 else NZ + lax.rem(z, 4)

    def c_copy(self, i, turn, arriving):
        q, z, core = self.q, self.z, self.core
        there = ring(z, i, NZ)
        sem = self.sems[2]
        slot = there if arriving else z
        return remote(
            self.cut.at[self.tile_of(there, turn)],
            self.recv_c.at[turn, slot],
            sem.at[0, turn, there],
            sem.at[1, turn, slot],
            device(q, there, core),
        )

    def b_to_c(self):
        self.recv_b[self.q] = self.half[self.q]

        @pl.loop(1, NQ)
        def _(i):
            self.b_copy(i, True).wait_recv()

        chunk = self.recv_b[0]
        for i in range(1, NQ):
            chunk = chunk + self.recv_b[i]
        across = self.lanes // 128
        for t in range(self.tiles):
            down, along = t // across, t % across
            self.cut[t] = chunk[
                down * self.high : (down + 1) * self.high, along * 128 : (along + 1) * 128
            ]

        @pl.loop(1, NZ)
        def _(i):
            for turn in range(self.rounds):
                self.c_copy(i, turn, False).start()

    def d_copy(self, i, turn, arriving):
        q, z, core = self.q, self.z, self.core
        sem = self.sems[3]
        if turn == 0:
            there = ring(z, i, NZ)
        else:
            there = lax.div(z, 4) * 4 + lax.rem(lax.rem(z, 4) + i, 4)
        slot = there if arriving else z
        tile = self.tile_of(slot, turn)
        return remote(
            self.joined.at[self.tile_of(z, turn)],
            self.joined.at[tile],
            sem.at[0, turn, there],
            sem.at[1, turn, slot],
            device(q, there, core),
        )

    def c_to_d(self):
        for turn in range(self.rounds):
            self.recv_c[turn, self.z] = self.cut[self.tile_of(self.z, turn)]

            @pl.loop(1, NZ)
            def _(i):
                self.c_copy(i, turn, True).wait_recv()

            tile = self.recv_c[turn, 0]
            for i in range(1, NZ):
                tile = tile + self.recv_c[turn, i]
            self.joined[self.tile_of(self.z, turn)] = tile

            @pl.loop(1, NZ if turn == 0 else 4)
            def _(i):
                self.d_copy(i, turn, False).start()

    def e_copy(self, i, arriving):
        q, z, core = self.q, self.z, self.core
        there = ring(q, i, NQ)
        sem = self.sems[4]
        slot = there if arriving else q
        return remote(
            self.total.at[core, q],
            self.total.at[core, slot],
            sem.at[0, there],
            sem.at[1, slot],
            device(there, z, core),
        )

    def f_copy(self, i, arriving):
        q, z, core = self.q, self.z, self.core
        at = ring(q, i, NQ)
        sem = self.sems[5]
        return remote(
            self.total.at[core, at],
            self.total.at[1 - core if arriving else core, at],
            sem.at[0, at],
            sem.at[1, at],
            device(q, z, 1 - core),
        )

    def d_to_e(self):
        for turn in range(self.rounds):

            @pl.loop(1, NZ if turn == 0 else 4)
            def _(i):
                self.d_copy(i, turn, True).wait_recv()

        across = self.lanes // 128
        for t in range(self.tiles):
            down, along = t // across, t % across
            self.total[
                self.core,
                self.q,
                down * self.high : (down + 1) * self.high,
                along * 128 : (along + 1) * 128,
            ] = self.joined[t]

        @pl.loop(1, NQ)
        def _(i):
            self.e_copy(i, False).start()

        self.f_copy(0, False).start()

    def e_to_f(self):
        @pl.loop(1, NQ)
        def _(i):
            self.e_copy(i, True).wait_recv()
            self.f_copy(i, False).start()

    def finish(self):
        @pl.loop(0, NQ)
        def _(i):
            self.f_copy(i, True).wait_recv()
            self.f_copy(i, False).wait_send()
            self.a_copy(i).wait_send()

        @pl.loop(1, NQ)
        def _(i):
            self.b_copy(i, False).wait_send()
            self.e_copy(i, False).wait_send()

        for turn in range(self.rounds):

            @pl.loop(1, NZ)
            def _(i):
                self.c_copy(i, turn, False).wait_send()

            @pl.loop(1, NZ if turn == 0 else 4)
            def _(i):
                self.d_copy(i, turn, False).wait_send()


def sum_scratch(rows, lanes, dtype):
    high = 16 if dtype == BF16 else 8
    tiles = (rows // high) * (lanes // 128)
    rounds = 2 if tiles > NZ else 1
    return [
        pltpu.VMEM((NQ, rows, lanes), dtype),
        pltpu.VMEM((NQ, rows, lanes), dtype),
        pltpu.VMEM((NQ, rows, lanes), dtype),
        pltpu.VMEM((tiles, high, 128), dtype),
        pltpu.VMEM((rounds, NZ, high, 128), dtype),
        pltpu.VMEM((tiles, high, 128), dtype),
        *STAGE_SEMS,
    ]


def fetch_kernel(owner_ref, tiles_ref, feat_ref, out_ref, part, *scratch):
    q, z, core = place()
    me = lax.axis_index("rows") * lax.axis_size("sub") + lax.axis_index("sub")
    rows = part.shape[2]
    per_tile = TILE // rows
    for s in range(STEPS):
        mine = jnp.full((rows, WIDTH), (owner_ref[s] == me).astype(F32)).astype(BF16)
        for t in range(BLOCK // TILE):
            tile = feat_ref[tiles_ref[s, t]]
            for i in range(per_tile):
                part[s, t * per_tile + i] = tile[i * rows : (i + 1) * rows] * mine
    greet(q, z, core)
    run = Sum(part, out_ref, *scratch[:6], scratch[6:], (q, z, core))
    run.start_a()
    run.a_to_b()
    run.b_to_c()
    run.c_to_d()
    run.d_to_e()
    run.e_to_f()
    run.finish()


def fetch_blocks(block_owner, block_tiles, features):
    rows = BLOCK // NQ
    shape = (STEPS, NQ, rows, WIDTH)
    out = pl.pallas_call(
        fetch_kernel,
        out_shape=jax.ShapeDtypeStruct(shape, BF16),
        in_specs=[smem(), smem(), vmem()],
        out_specs=vmem(),
        scratch_shapes=[pltpu.VMEM(shape, BF16), *sum_scratch(rows, WIDTH, BF16)],
        compiler_params=pltpu.CompilerParams(
            collective_id=0, has_side_effects=True, vmem_limit_bytes=VMEM_BYTES
        ),
        name="fetch_blocks",
    )(block_owner, block_tiles, features.reshape(-1, TILE, WIDTH))
    return out.reshape(STEPS * BLOCK, WIDTH)


LOG2E_SCALED = math.log2(math.e) / WIDTH


def column_norms(rows):
    wide = rows.astype(F32)
    return jnp.sum(wide * wide, axis=1, keepdims=True)


def slab_kernel(block_ref, feat_ref, res_ref, coef_ref, slab_ref, part_ref, norm_ref):
    @pl.when(pl.program_id(0) == 0)
    def _():
        norm = column_norms(block_ref[...]) * LOG2E_SCALED
        norm_ref[...] = jnp.broadcast_to(norm, norm_ref.shape)
        part_ref[...] = jnp.zeros_like(part_ref)

    feat = feat_ref[...]
    norms = column_norms(feat) * LOG2E_SCALED
    along = jnp.transpose(jnp.broadcast_to(norms, (CHUNK, 128)))[0:1, :]
    weighted = (res_ref[...] - RIDGE * coef_ref[...]).astype(BF16)
    slabs = []
    for s in range(STEPS):
        at = pl.ds(s * BLOCK, BLOCK)
        cross = dot_nt(block_ref[at, :], feat)
        power = (2.0 * LOG2E_SCALED) * cross - along - norm_ref[at, 0:1]
        slab = jnp.exp2(power).astype(BF16)
        slab_ref[at, :] = slab
        slabs.append(slab)
        part_ref[:, s * TARGETS : (s + 1) * TARGETS] += dot(slab, weighted)
    part_ref[:, STEPS * TARGETS :] += dot_nt(slabs[1], slabs[0])


def slab_parts(blocks, features, residual, coefficients):
    rows = features.shape[0]
    return pl.pallas_call(
        slab_kernel,
        grid=(rows // CHUNK,),
        out_shape=(
            jax.ShapeDtypeStruct((STEPS * BLOCK, rows), BF16),
            jax.ShapeDtypeStruct((BLOCK, STEPS * TARGETS + BLOCK), F32),
        ),
        in_specs=[
            pl.BlockSpec((STEPS * BLOCK, WIDTH), lambda i: (0, 0)),
            pl.BlockSpec((CHUNK, WIDTH), lambda i: (i, 0)),
            pl.BlockSpec((CHUNK, TARGETS), lambda i: (i, 0)),
            pl.BlockSpec((CHUNK, TARGETS), lambda i: (i, 0)),
        ],
        out_specs=(
            pl.BlockSpec((STEPS * BLOCK, CHUNK), lambda i: (0, i)),
            pl.BlockSpec((BLOCK, STEPS * TARGETS + BLOCK), lambda i: (0, 0)),
        ),
        scratch_shapes=[pltpu.VMEM((STEPS * BLOCK, 128), F32)],
        compiler_params=pltpu.CompilerParams(vmem_limit_bytes=VMEM_BYTES),
        name="slab_parts",
    )(blocks, features, residual, coefficients)


PANEL = 4


def invert_tile(mats):
    n = TILE
    row = lax.broadcasted_iota(jnp.int32, (n, n), 0)
    lane = lax.broadcasted_iota(jnp.int32, (n, n), 1)
    mats = list(mats)
    for first in range(0, n, PANEL):
        columns = [
            [jnp.broadcast_to(a[:, first + j : first + j + 1], (n, n)) for j in range(PANEL)]
            for a in mats
        ]
        for j in range(PANEL):
            k = first + j
            for m, a in enumerate(mats):
                column = columns[m][j]
                inverse = 1.0 / column[k : k + 1, :]
                column = jnp.where(row == k, column - 1.0, column)
                a = jnp.where(lane == k, jnp.where(row == k, 1.0, 0.0), a)
                mats[m] = a - column * (a[k : k + 1, :] * inverse)
                for jj in range(j + 1, PANEL):
                    other = columns[m][jj]
                    columns[m][jj] = other - column * (other[k : k + 1, :] * inverse)
    return mats


def invert_kernel(block_ref, inv_ref, between_ref):
    blocks = block_ref[...]
    norms = column_norms(blocks) * LOG2E_SCALED
    along = jnp.transpose(jnp.broadcast_to(norms, (STEPS * BLOCK, 128)))[0:1, :]
    row = lax.broadcasted_iota(jnp.int32, (BLOCK, BLOCK), 0)
    lane = lax.broadcasted_iota(jnp.int32, (BLOCK, BLOCK), 1)

    def kernel(left, right):
        a, b = left * BLOCK, right * BLOCK
        cross = dot_nt(blocks[a : a + BLOCK], blocks[b : b + BLOCK])
        return jnp.exp2(
            (2.0 * LOG2E_SCALED) * cross - along[:, b : b + BLOCK] - norms[a : a + BLOCK]
        )

    for s in range(STEPS):
        inv_ref[s] = kernel(s, s) + jnp.where(row == lane, RIDGE, 0.0)
    between_ref[...] = kernel(1, 0).astype(BF16)

    def eliminate(k, carry):
        at = pl.ds(pl.multiple_of(k * TILE, TILE), TILE)
        tiles = invert_tile([inv_ref[s, at, at] for s in range(STEPS)])
        inside = lax.div(lax.broadcasted_iota(jnp.int32, (TILE, BLOCK), 1), TILE) == k
        for s in range(STEPS):
            lead = dot(tiles[s], inv_ref[s, at, :], HI)
            lead = jnp.where(inside, jnp.concatenate([tiles[s]] * (BLOCK // TILE), axis=1), lead)
            column = inv_ref[s, :, at]
            inv_ref[s, :, at] = jnp.zeros_like(column)
            inv_ref[s] -= dot(column, lead, HI)
            inv_ref[s, at, :] = lead
        return carry

    lax.fori_loop(0, BLOCK // TILE, eliminate, 0)


def invert_blocks(blocks):
    return pl.pallas_call(
        invert_kernel,
        out_shape=(
            jax.ShapeDtypeStruct((STEPS, BLOCK, BLOCK), F32),
            jax.ShapeDtypeStruct((BLOCK, BLOCK), BF16),
        ),
        in_specs=[vmem()],
        out_specs=(vmem(), vmem()),
        compiler_params=pltpu.CompilerParams(vmem_limit_bytes=VMEM_BYTES),
        name="invert_blocks",
    )(blocks)


def reduce_kernel(part_ref, out_ref, *scratch):
    spot = place()
    greet(*spot)
    run = Sum(part_ref, out_ref, *scratch[:6], scratch[6:], spot)
    run.start_a()
    run.a_to_b()
    run.b_to_c()
    run.c_to_d()
    run.d_to_e()
    run.e_to_f()
    run.finish()


def reduce_parts(parts):
    height, lanes = parts.shape
    rows = height // (2 * NQ)
    shape = (2, NQ, rows, lanes)
    out = pl.pallas_call(
        reduce_kernel,
        out_shape=jax.ShapeDtypeStruct(shape, F32),
        in_specs=[vmem()],
        out_specs=vmem(),
        scratch_shapes=sum_scratch(rows, lanes, F32),
        compiler_params=pltpu.CompilerParams(
            collective_id=1, has_side_effects=True, vmem_limit_bytes=VMEM_BYTES
        ),
        name="reduce_parts",
    )(parts.reshape(shape))
    return out.reshape(height, lanes)


def final_kernel(
    step_size,
    owner_ref,
    tiles_ref,
    sum_ref,
    inv_ref,
    between_ref,
    slab_ref,
    res_ref,
    coef_ref,
    res_out,
    coef_out,
    update_ref,
    low_ref,
):
    step = pl.program_id(0)

    @pl.when(step == 0)
    def _():
        first = dot(inv_ref[0], sum_ref[:, :TARGETS], HI) * step_size
        first_low = first.astype(BF16)
        gradient = (
            sum_ref[:, TARGETS : 2 * TARGETS]
            - dot(sum_ref[:, 2 * TARGETS :], first_low.astype(F32), HI)
            - RIDGE * dot(between_ref[...].astype(F32), first, HI)
        )
        second = dot(inv_ref[1], gradient, HI) * step_size
        update_ref[0:BLOCK] = first
        update_ref[BLOCK:] = second
        low_ref[...] = jnp.transpose(update_ref[...]).astype(BF16)

    res_out[...] = res_ref[...] - jnp.transpose(dot(low_ref[...], slab_ref[...]))
    coef_out[...] = coef_ref[...]
    me = lax.axis_index("rows") * lax.axis_size("sub") + lax.axis_index("sub")
    tiles_here = CHUNK // TILE
    for s in range(STEPS):
        for t in range(BLOCK // TILE):
            tile = tiles_ref[s, t]

            @pl.when((owner_ref[s] == me) & (lax.div(tile, tiles_here) == step))
            def _():
                at = pl.ds(pl.multiple_of(lax.rem(tile, tiles_here) * TILE, TILE), TILE)
                coef_out[at, :] += update_ref[pl.ds(s * BLOCK + t * TILE, TILE), :]


def final(step_size, owner, tiles, sums, inverses, between, slabs, residual, coefficients):
    rows = residual.shape[0]
    whole2 = lambda i: (0, 0)
    chunk = pl.BlockSpec((CHUNK, TARGETS), lambda i: (i, 0))
    return pl.pallas_call(
        functools.partial(final_kernel, step_size),
        grid=(rows // CHUNK,),
        out_shape=(
            jax.ShapeDtypeStruct(residual.shape, F32),
            jax.ShapeDtypeStruct(coefficients.shape, F32),
        ),
        in_specs=[
            smem(),
            smem(),
            pl.BlockSpec(sums.shape, whole2),
            pl.BlockSpec(inverses.shape, lambda i: (0, 0, 0)),
            pl.BlockSpec(between.shape, whole2),
            pl.BlockSpec((STEPS * BLOCK, CHUNK), lambda i: (0, i)),
            chunk,
            chunk,
        ],
        out_specs=(chunk, chunk),
        scratch_shapes=[
            pltpu.VMEM((STEPS * BLOCK, TARGETS), F32),
            pltpu.VMEM((TARGETS, STEPS * BLOCK), BF16),
        ],
        compiler_params=pltpu.CompilerParams(vmem_limit_bytes=VMEM_BYTES),
        name="final",
    )(owner, tiles, sums, inverses, between, slabs, residual, coefficients)


def local(features, residual, coefficients, block_owner, block_tiles):
    devices = lax.axis_size("rows") * lax.axis_size("sub")
    step_size = 1.0 / math.sqrt(features.shape[0] * devices)
    blocks = fetch_blocks(block_owner, block_tiles, features)
    slabs, parts = slab_parts(blocks, features, residual, coefficients)
    sums = reduce_parts(parts)
    inverses, between = invert_blocks(blocks)
    return final(
        step_size,
        block_owner,
        block_tiles,
        sums,
        inverses,
        between,
        slabs,
        residual,
        coefficients,
    )


def solution(mesh):
    in_specs = (
        P(("rows", "sub"), None),
        P(("rows", "sub"), None),
        P(("rows", "sub"), None),
        P(),
        P(),
    )
    out_specs = (P(("rows", "sub"), None), P(("rows", "sub"), None))
    return jax.shard_map(local, mesh=mesh, in_specs=in_specs, out_specs=out_specs, check_vma=False)
```

time: 938 us -> 163 us (0.17); the launches traced: 927 us -> 163 us
  waiting for transfers between devices: 555 us -> 0 us
  other arithmetic: 252 us -> 0 us
  Pallas kernels: 0 us -> 162 us
  matrix products: 58.9 us -> 0 us
  local copies, waits for them, and re-layouts: 39.3 us -> 0 us
  between operations: 21.1 us -> 0.65 us
    psum x3 -> x0, waiting for transfers between devices: 555 us -> none  [the longest x2 299 us: local(): gradient = lax.psum(local_term, ('rows', 'sub'))]
    another operation x35 -> x0, other arithmetic: 241 us -> none  [the longest x30 159 us: block_solve(): factor = jnp.linalg.cholesky(system)]
    pallas_call x0 -> x5, Pallas kernels: none -> 162 us  [the longest x1 44.4 us: fetch_blocks(): pl.pallas_call(fetch_kernel, out_shape=jax.ShapeDtypeStruct(shape, BF16),...]
    dot_general x8 -> x0, matrix products: 30.4 us -> none  [the longest x4 14.8 us: kernel_slab(): jnp.einsum('rf,bf->rb', left_rows, right_rows, preferred_element_type=jnp...]
    another operation x40 -> x0, matrix products: 28.5 us -> none  [the longest x12 10.9 us: block_solve(): factor = jnp.linalg.cholesky(system)]
    another operation x35 -> x0, local copies, waits for them, and re-layouts: 22.7 us -> none  [the longest x27 22.4 us: block_solve(): lax.linalg.triangular_solve(factor, half_way, left_side=True, lower=True,...]
  transfers between devices with their start and end apart: 3 -> 0, of which waited for: 3 -> 0; matrix products, arithmetic and copies ran while one was open for 21% -> 0% of each run, Pallas kernels for 0% -> 0%
where the time goes in v1:
time: 163 us
  Pallas kernels  162 us (99%)
    pallas_call x1, Pallas kernels, fetch_blocks(): pl.pallas_call(fetch_kernel, out_shape=jax.ShapeDtypeStruct(shape, BF16),...  44.4 us
    pallas_call x1, Pallas kernels, reduce_parts(): pl.pallas_call(reduce_kernel, out_shape=jax.ShapeDtypeStruct(shape, F32),...  44.1 us
    pallas_call x1, Pallas kernels, invert_blocks(): pl.pallas_call(invert_kernel, out_shape=(jax.ShapeDtypeStruct((STEPS, BLO...  42.4 us
    pallas_call x1, Pallas kernels, final(): pl.pallas_call(functools.partial(final_kernel, step_size), grid=(rows //...  16.7 us
    pallas_call x1, Pallas kernels, slab_parts(): pl.pallas_call(slab_kernel, grid=(rows // CHUNK,), out_shape=(jax.ShapeDt...  14.9 us

profile of v1, /device:TPU:1, one launch (start us, length us, event | category | flops | bytes accessed | tf_op | source)
XLA Modules:
  0.0 163.0 jit_solution(14785998976073706110)
XLA Ops:
  0.6 44.4 %fetch_blocks.1 = bf16[2,16,32,512]{3,2,1,0:T(8,128)(2,1)} custom-call(s32[2]{0:T(128)} %owner_ref.3, s32[2,4]{1,0:T(2,128)} %tiles_ref.3, bf16[32,128,512]{2,1,0:T(8,128)(2,1)} %bitcast.4), custom_call_target="tpu_custom_call" | custom-call | tf_op jit(solution)/shard_map/fetch_blocks/pallas_call | solution.py:345
  45.1 42.4 %invert_blocks.1 = (f32[2,512,512]{2,1,0:T(8,128)}, bf16[512,512]{1,0:T(8,128)(2,1)}) custom-call(bf16[1024,512]{1,0:T(8,128)(2,1)} %bitcast.5), custom_call_target="tpu_custom_call" | custom-call | tf_op jit(solution)/shard_map/invert_blocks/pallas_call | solution.py:477
  87.4 14.9 %slab_parts.1 = (bf16[1024,4096]{1,0:T(8,128)(2,1)}, f32[512,768]{1,0:T(8,128)}) custom-call(bf16[1024,512]{1,0:T(8,128)(2,1)} %bitcast.6, bf16[4096,512]{1,0:T(8,128)(2,1)} %feat_ref.1, f32[4096,128]{1,0:T(8,128)} %res_ref.3, f32[4096,128]{1,0:T(8,128)} %coef_ref.3), custom_call_target="tpu_custom_call" | custom-call | tf_op jit(solution)/shard_map/slab_parts/pallas_call | solution.py:392
  102.3 44.1 %reduce_parts.1 = f32[2,16,16,768]{3,2,1,0:T(8,128)} custom-call(f32[2,16,16,768]{3,2,1,0:T(8,128)} %bitcast.8), custom_call_target="tpu_custom_call" | custom-call | tf_op jit(solution)/shard_map/reduce_parts/pallas_call | solution.py:507
  146.4 16.7 %final.1 = (f32[4096,128]{1,0:T(8,128)}, f32[4096,128]{1,0:T(8,128)}) custom-call(s32[2]{0:T(128)} %owner_ref.3, s32[2,4]{1,0:T(2,128)} %tiles_ref.3, f32[512,768]{1,0:T(8,128)} %bitcast.7, f32[2,512,512]{2,1,0:T(8,128)} %get-tuple-element.7.inv_ref, bf16[512,512]{1,0:T(8,128)(2,1)} %get-tuple-element.8.between_ref, ...), custom_call_target="tpu_custom_call" | custom-call | tf_op jit(solution)/shard_map/final/pallas_call | solution.py:570

commit v2 on v0

v2 whole, which is shorter than its diff:
```python
import functools
import math

import jax
import jax.numpy as jnp
from jax import lax
from jax.experimental import pallas as pl
from jax.experimental.pallas import tpu as pltpu
from jax.sharding import PartitionSpec as P

MESH = pl.DeviceIdType.MESH
HI = lax.Precision.HIGHEST
F32 = jnp.float32
BF16 = jnp.bfloat16

BLOCK = 512
TILE = 128
STEPS = 2
RIDGE = 0.5
WIDTH = 512
TARGETS = 128
NX, NY, NZ = 4, 4, 8
NQ = NX * NY
CHUNK = 1024


def vmem():
    return pl.BlockSpec(memory_space=pltpu.VMEM)


def smem():
    return pl.BlockSpec(memory_space=pltpu.SMEM)


def dot(a, b, precision=None):
    return jnp.dot(a, b, precision=precision, preferred_element_type=F32)


def dot_nt(a, b, precision=None):
    return lax.dot_general(
        a, b, (((1,), (1,)), ((), ())), precision=precision, preferred_element_type=F32
    )


def place():
    across, within = lax.axis_index("rows"), lax.axis_index("sub")
    core = lax.rem(across, 2)
    y = lax.rem(lax.div(across, 2), NY)
    z = lax.div(across, 2 * NY) * 2 + lax.rem(within, 2)
    x = lax.div(within, 2)
    return x, y, z, core


def device(x, y, z, core):
    return (lax.div(z, 2) * (2 * NY) + y * 2 + core, x * 2 + lax.rem(z, 2))


def around(at, step, size):
    return lax.rem(at + step, size)


def hops(step, size):
    return min(step, size - step)


COLUMNS = sorted(
    [(i, j) for i in range(NX) for j in range(NY) if i or j],
    key=lambda s: -hops(s[0], NX) - hops(s[1], NY),
)
PLANES = sorted(range(1, NZ), key=lambda s: -hops(s, NZ))


def greet(spot):
    x, y, z, core = spot
    barrier = pltpu.get_barrier_semaphore()

    def signal(*where):
        pl.semaphore_signal(barrier, inc=1, device_id=device(*where), device_id_type=MESH)

    for i, j in COLUMNS:
        signal(around(x, i, NX), around(y, j, NY), z, core)
    for k in PLANES:
        signal(x, y, around(z, k, NZ), core)
    signal(x, y, z, 1 - core)
    pl.semaphore_wait(barrier, 1 + len(COLUMNS) + len(PLANES))


def remote(source, target, send_sem, recv_sem, where):
    return pltpu.make_async_remote_copy(
        src_ref=source,
        dst_ref=target,
        send_sem=send_sem,
        recv_sem=recv_sem,
        device_id=device(*where),
        device_id_type=MESH,
    )


NCOL = len(COLUMNS)


class Sum:
    def __init__(self, part, total, recv_a, half, recv_b, recv_c, sems, spot):
        self.part, self.total, self.recv_a, self.half = part, total, recv_a, half
        self.recv_b, self.recv_c = recv_b, recv_c
        self.sems = sems
        self.x, self.y, self.z, self.core = spot
        self.q = self.x * NY + self.y
        self.mate = (self.x, self.y, self.z, 1 - self.core)

    def column(self, i):
        dx, dy = COLUMNS[i] if i < NCOL else (0, 0)
        x, y = around(self.x, dx, NX), around(self.y, dy, NY)
        return (x, y, self.z, self.core), x * NY + y

    def column_before(self, i):
        dx, dy = COLUMNS[i] if i < NCOL else (0, 0)
        return around(self.x, NX - dx, NX) * NY + around(self.y, NY - dy, NY)

    def a_copy(self, i):
        at = self.column(i)[1]
        sem = self.sems[0]
        return remote(
            self.part.at[1 - self.core, at], self.recv_a.at[i], sem.at[0, i], sem.at[1, i], self.mate
        )

    def start_a(self):
        for i in range(NQ):
            self.a_copy(i).start()

    def b_copy(self, i):
        sem = self.sems[1]
        return remote(
            self.half.at[i], self.recv_b.at[i], sem.at[0, i], sem.at[1, i], self.column(i)[0]
        )

    def a_to_b(self):
        for i in range(NQ):
            at = self.column(i)[1]
            self.a_copy(i).wait_recv()
            self.half[i] = self.part[self.core, at] + self.recv_a[i]
            if i < NCOL:
                self.b_copy(i).start()

    def c_copy(self, i, slot):
        sem = self.sems[2]
        there = around(self.z, PLANES[i], NZ)
        return remote(
            self.recv_c.at[self.z],
            self.recv_c.at[slot],
            sem.at[0, i],
            sem.at[1, i],
            (self.x, self.y, there, self.core),
        )

    def b_to_c(self):
        chunk = self.half[NCOL]
        for i in reversed(range(NCOL)):
            self.b_copy(i).wait_recv()
            chunk = chunk + self.recv_b[i]
        self.recv_c[self.z] = chunk
        for i in range(len(PLANES)):
            self.c_copy(i, self.z).start()

    def e_copy(self, i, slot):
        sem = self.sems[3]
        return remote(
            self.total.at[self.core, self.q],
            self.total.at[self.core, slot],
            sem.at[0, i],
            sem.at[1, i],
            self.column(i)[0],
        )

    def f_copy(self, i, side):
        at = self.column_before(i)
        sem = self.sems[4]
        return remote(
            self.total.at[self.core, at],
            self.total.at[side, at],
            sem.at[0, i],
            sem.at[1, i],
            self.mate,
        )

    def c_to_e(self):
        for i in range(len(PLANES)):
            self.c_copy(i, around(self.z, NZ - PLANES[i], NZ)).wait_recv()
        chunk = self.recv_c[0]
        for i in range(1, NZ):
            chunk = chunk + self.recv_c[i]
        self.total[self.core, self.q] = chunk
        for i in range(NCOL):
            self.e_copy(i, self.q).start()
        self.f_copy(NCOL, self.core).start()

    def e_to_f(self):
        for i in reversed(range(NCOL)):
            self.e_copy(i, self.column_before(i)).wait_recv()
            self.f_copy(i, self.core).start()

    def finish(self):
        for i in reversed(range(NQ)):
            self.f_copy(i, 1 - self.core).wait_recv()
        for i in range(NQ):
            self.a_copy(i).wait_send()
            self.f_copy(i, self.core).wait_send()
        for i in range(NCOL):
            self.b_copy(i).wait_send()
            self.e_copy(i, self.q).wait_send()
        for i in range(len(PLANES)):
            self.c_copy(i, self.z).wait_send()


def sum_scratch(rows, lanes, dtype):
    return [
        pltpu.VMEM((NQ, rows, lanes), dtype),
        pltpu.VMEM((NQ, rows, lanes), dtype),
        pltpu.VMEM((NCOL, rows, lanes), dtype),
        pltpu.VMEM((NZ, rows, lanes), dtype),
        pltpu.SemaphoreType.DMA((2, NQ)),
        pltpu.SemaphoreType.DMA((2, NCOL)),
        pltpu.SemaphoreType.DMA((2, len(PLANES))),
        pltpu.SemaphoreType.DMA((2, NCOL)),
        pltpu.SemaphoreType.DMA((2, NQ)),
    ]


def fetch_kernel(owner_ref, tiles_ref, feat_hbm, out_ref, feat_ref, feat_sem, part, *scratch):
    load = pltpu.make_async_copy(feat_hbm, feat_ref, feat_sem)
    load.start()
    spot = place()
    core = spot[3]
    greet(spot)
    load.wait()
    me = lax.axis_index("rows") * lax.axis_size("sub") + lax.axis_index("sub")
    rows = part.shape[2]
    per_tile = TILE // rows
    run = Sum(part, out_ref, *scratch[:4], scratch[4:], spot)

    def build(s):
        mine = jnp.full((rows, WIDTH), (owner_ref[s] == me).astype(F32)).astype(BF16)
        for t in range(BLOCK // TILE):
            tile = feat_ref[tiles_ref[s, t]]
            for i in range(per_tile):
                part[s, t * per_tile + i] = tile[i * rows : (i + 1) * rows] * mine

    build(1 - core)
    run.start_a()
    build(core)
    run.a_to_b()
    run.b_to_c()
    run.c_to_e()
    run.e_to_f()
    run.finish()


def fetch_blocks(block_owner, block_tiles, features):
    rows = BLOCK // NQ
    shape = (STEPS, NQ, rows, WIDTH)
    tiled = features.reshape(-1, TILE, WIDTH)
    out = pl.pallas_call(
        fetch_kernel,
        out_shape=jax.ShapeDtypeStruct(shape, BF16),
        in_specs=[smem(), smem(), pl.BlockSpec(memory_space=pl.ANY)],
        out_specs=vmem(),
        scratch_shapes=[
            pltpu.VMEM(tiled.shape, BF16),
            pltpu.SemaphoreType.DMA,
            pltpu.VMEM(shape, BF16),
            *sum_scratch(rows, WIDTH, BF16),
        ],
        compiler_params=pltpu.CompilerParams(
            collective_id=0, has_side_effects=True, vmem_limit_bytes=16 << 20
        ),
        name="fetch_blocks",
    )(block_owner, block_tiles, tiled)
    return out.reshape(STEPS * BLOCK, WIDTH)


LOG2E_SCALED = math.log2(math.e) / WIDTH


def column_norms(rows):
    wide = rows.astype(F32)
    return jnp.sum(wide * wide, axis=1, keepdims=True)


def slab_kernel(block_ref, feat_ref, res_ref, coef_ref, slab_ref, part_ref, norm_ref):
    @pl.when(pl.program_id(0) == 0)
    def _():
        norm = column_norms(block_ref[...]) * LOG2E_SCALED
        norm_ref[...] = jnp.broadcast_to(norm, norm_ref.shape)
        part_ref[...] = jnp.zeros_like(part_ref)

    feat = feat_ref[...]
    norms = column_norms(feat) * LOG2E_SCALED
    along = jnp.transpose(jnp.broadcast_to(norms, (CHUNK, 128)))[0:1, :]
    weighted = (res_ref[...] - RIDGE * coef_ref[...]).astype(BF16)
    slabs = []
    for s in range(STEPS):
        at = pl.ds(s * BLOCK, BLOCK)
        cross = dot_nt(block_ref[at, :], feat)
        power = (2.0 * LOG2E_SCALED) * cross - along - norm_ref[at, 0:1]
        slab = jnp.exp2(power).astype(BF16)
        slab_ref[at, :] = slab
        slabs.append(slab)
        part_ref[:, s * TARGETS : (s + 1) * TARGETS] += dot(slab, weighted)
    part_ref[:, STEPS * TARGETS :] += dot_nt(slabs[1], slabs[0])


def slab_parts(blocks, features, residual, coefficients):
    rows = features.shape[0]
    return pl.pallas_call(
        slab_kernel,
        grid=(rows // CHUNK,),
        out_shape=(
            jax.ShapeDtypeStruct((STEPS * BLOCK, rows), BF16),
            jax.ShapeDtypeStruct((BLOCK, STEPS * TARGETS + BLOCK), F32),
        ),
        in_specs=[
            pl.BlockSpec((STEPS * BLOCK, WIDTH), lambda i: (0, 0)),
            pl.BlockSpec((CHUNK, WIDTH), lambda i: (i, 0)),
            pl.BlockSpec((CHUNK, TARGETS), lambda i: (i, 0)),
            pl.BlockSpec((CHUNK, TARGETS), lambda i: (i, 0)),
        ],
        out_specs=(
            pl.BlockSpec((STEPS * BLOCK, CHUNK), lambda i: (0, i)),
            pl.BlockSpec((BLOCK, STEPS * TARGETS + BLOCK), lambda i: (0, 0)),
        ),
        scratch_shapes=[pltpu.VMEM((STEPS * BLOCK, 128), F32)],
        compiler_params=pltpu.CompilerParams(vmem_limit_bytes=28 << 20),
        name="slab_parts",
    )(blocks, features, residual, coefficients)


PANEL = 4
HALF_TILE = TILE // 2


def eliminate(a, begin, end):
    n = TILE
    row = lax.broadcasted_iota(jnp.int32, (n, n), 0)
    lane = lax.broadcasted_iota(jnp.int32, (n, n), 1)
    for first in range(begin, end, PANEL):
        columns = [
            jnp.broadcast_to(a[:, first + j : first + j + 1], (n, n)) for j in range(PANEL)
        ]
        for j in range(PANEL):
            k = first + j
            column = columns[j]
            inverse = 1.0 / column[k : k + 1, :]
            column = jnp.where(row == k, column - 1.0, column)
            a = jnp.where(lane == k, jnp.where(row == k, 1.0, 0.0), a)
            a = a - column * (a[k : k + 1, :] * inverse)
            for jj in range(j + 1, PANEL):
                other = columns[jj]
                columns[jj] = other - column * (other[k : k + 1, :] * inverse)
    return a


def split3(wide):
    high = wide.astype(BF16)
    rest = wide - high.astype(F32)
    middle = rest.astype(BF16)
    low = (rest - middle.astype(F32)).astype(BF16)
    return high, middle, low


def product(left, right):
    lh, lm, ll = left
    rh, rm, rl = right
    small = dot(lh, rl) + dot(lm, rm) + dot(ll, rh)
    return dot(lh, rh) + (dot(lh, rm) + dot(lm, rh) + small)


def solve_kernel(
    step_size,
    block_ref,
    part_ref,
    update_ref,
    low_ref,
    total,
    inv,
    thirds,
    between,
    swap_sem,
    *scratch,
):
    spot = place()
    core = spot[3]
    greet(spot)
    run = Sum(part_ref, total, *scratch[:4], scratch[4:], spot)
    run.start_a()

    def block(s):
        return block_ref[pl.ds(pl.multiple_of(s * BLOCK, BLOCK), BLOCK), :]

    def kernel(left, right):
        a = column_norms(left) * LOG2E_SCALED
        b = column_norms(right) * LOG2E_SCALED
        along = jnp.transpose(jnp.broadcast_to(b, (BLOCK, TILE)))[0:1, :]
        return jnp.exp2((2.0 * LOG2E_SCALED) * dot_nt(left, right) - along - a)

    own = block(core)
    row = lax.broadcasted_iota(jnp.int32, (BLOCK, BLOCK), 0)
    lane = lax.broadcasted_iota(jnp.int32, (BLOCK, BLOCK), 1)
    inv[core] = kernel(own, own) + jnp.where(row == lane, RIDGE, 0.0)
    between[...] = kernel(block(1), block(0)).astype(BF16)

    stages = {0: run.a_to_b, 3: run.b_to_c, 5: run.c_to_e, 7: run.e_to_f}

    def hook(k, half):
        for at, stage in stages.items():
            if at % 2 == half:
                pl.when(k == at // 2)(stage)

    def step(k, carry):
        at = pl.ds(pl.multiple_of(k * TILE, TILE), TILE)
        inv[core, at, at] = eliminate(inv[core, at, at], 0, HALF_TILE)
        hook(k, 0)
        tile = eliminate(inv[core, at, at], HALF_TILE, TILE)
        inside = lax.div(lax.broadcasted_iota(jnp.int32, (TILE, BLOCK), 1), TILE) == k
        lead = dot(tile, inv[core, at, :], HI)
        lead = jnp.where(inside, jnp.concatenate([tile] * (BLOCK // TILE), axis=1), lead)
        column = inv[core, :, at]
        inv[core, :, at] = jnp.zeros_like(column)
        inv[core] -= dot(column, lead, HI)
        inv[core, at, :] = lead
        hook(k, 1)
        return carry

    lax.fori_loop(0, BLOCK // TILE, step, 0)

    def swap(side):
        return remote(inv.at[core], inv.at[side], swap_sem.at[0], swap_sem.at[1], run.mate)

    swap(core).start()
    swap(1 - core).wait_recv()
    for s in range(STEPS):
        for i, third in enumerate(split3(inv[s])):
            thirds[s, i] = third
    run.finish()

    sums = total[...].reshape(BLOCK, total.shape[3])
    both = [(thirds[s, 0], thirds[s, 1], thirds[s, 2]) for s in range(STEPS)]
    first = product(both[0], split3(sums[:, :TARGETS])) * step_size
    first_low = first.astype(BF16)
    shift = sum(dot(third, first_low) for third in split3(sums[:, STEPS * TARGETS :]))
    past = sum(dot(between[...], third) for third in split3(first))
    gradient = sums[:, TARGETS : STEPS * TARGETS] - shift - RIDGE * past
    second = product(both[1], split3(gradient)) * step_size
    update_ref[0:BLOCK] = first
    update_ref[BLOCK:] = second
    low_ref[:, 0:BLOCK] = jnp.transpose(first).astype(BF16)
    low_ref[:, BLOCK:] = jnp.transpose(second).astype(BF16)
    swap(core).wait_send()


def solve(step_size, blocks, parts):
    height, lanes = parts.shape
    rows = height // (2 * NQ)
    shape = (2, NQ, rows, lanes)
    return pl.pallas_call(
        functools.partial(solve_kernel, step_size),
        out_shape=(
            jax.ShapeDtypeStruct((STEPS * BLOCK, TARGETS), F32),
            jax.ShapeDtypeStruct((TARGETS, STEPS * BLOCK), BF16),
        ),
        in_specs=[vmem(), vmem()],
        out_specs=(vmem(), vmem()),
        scratch_shapes=[
            pltpu.VMEM(shape, F32),
            pltpu.VMEM((STEPS, BLOCK, BLOCK), F32),
            pltpu.VMEM((STEPS, 3, BLOCK, BLOCK), BF16),
            pltpu.VMEM((BLOCK, BLOCK), BF16),
            pltpu.SemaphoreType.DMA((2,)),
            *sum_scratch(rows, lanes, F32),
        ],
        compiler_params=pltpu.CompilerParams(
            collective_id=1, has_side_effects=True, vmem_limit_bytes=28 << 20
        ),
        name="solve",
    )(blocks, parts.reshape(shape))


ROWS_STEP = 1024


def final_kernel(
    owner_ref, tiles_ref, update_ref, low_ref, slab_ref, res_ref, coef_ref, res_out, coef_out
):
    step = pl.program_id(0)
    res_out[...] = res_ref[...] - jnp.transpose(dot(low_ref[...], slab_ref[...]))
    coef_out[...] = coef_ref[...]
    me = lax.axis_index("rows") * lax.axis_size("sub") + lax.axis_index("sub")
    tiles_here = ROWS_STEP // TILE
    for s in range(STEPS):
        for t in range(BLOCK // TILE):
            tile = tiles_ref[s, t]

            @pl.when((owner_ref[s] == me) & (lax.div(tile, tiles_here) == step))
            def _():
                at = pl.ds(pl.multiple_of(lax.rem(tile, tiles_here) * TILE, TILE), TILE)
                coef_out[at, :] += update_ref[pl.ds(s * BLOCK + t * TILE, TILE), :]


def final(owner, tiles, updates, low, slabs, residual, coefficients):
    rows = residual.shape[0]
    whole = lambda i: (0, 0)
    chunk = pl.BlockSpec((ROWS_STEP, TARGETS), lambda i: (i, 0))
    return pl.pallas_call(
        final_kernel,
        grid=(rows // ROWS_STEP,),
        out_shape=(
            jax.ShapeDtypeStruct(residual.shape, F32),
            jax.ShapeDtypeStruct(coefficients.shape, F32),
        ),
        in_specs=[
            smem(),
            smem(),
            pl.BlockSpec(updates.shape, whole),
            pl.BlockSpec(low.shape, whole),
            pl.BlockSpec((STEPS * BLOCK, ROWS_STEP), lambda i: (0, i)),
            chunk,
            chunk,
        ],
        out_specs=(chunk, chunk),
        compiler_params=pltpu.CompilerParams(vmem_limit_bytes=16 << 20),
        name="final",
    )(owner, tiles, updates, low, slabs, residual, coefficients)


def local(features, residual, coefficients, block_owner, block_tiles):
    devices = lax.axis_size("rows") * lax.axis_size("sub")
    step_size = 1.0 / math.sqrt(features.shape[0] * devices)
    blocks = fetch_blocks(block_owner, block_tiles, features)
    slabs, parts = slab_parts(blocks, features, residual, coefficients)
    updates, low = solve(step_size, blocks, parts)
    return final(block_owner, block_tiles, updates, low, slabs, residual, coefficients)


def solution(mesh):
    in_specs = (
        P(("rows", "sub"), None),
        P(("rows", "sub"), None),
        P(("rows", "sub"), None),
        P(),
        P(),
    )
    out_specs = (P(("rows", "sub"), None), P(("rows", "sub"), None))
    return jax.shard_map(local, mesh=mesh, in_specs=in_specs, out_specs=out_specs, check_vma=False)
```

time: 938 us -> 113 us (0.12); the launches traced: 927 us -> 112 us
  waiting for transfers between devices: 555 us -> 0 us
  other arithmetic: 252 us -> 0 us
  Pallas kernels: 0 us -> 105 us
  matrix products: 58.9 us -> 0 us
  local copies, waits for them, and re-layouts: 39.3 us -> 6.71 us
  between operations: 21.1 us -> 0.71 us
    psum x3 -> x0, waiting for transfers between devices: 555 us -> none  [the longest x2 299 us: local(): gradient = lax.psum(local_term, ('rows', 'sub'))]
    another operation x35 -> x0, other arithmetic: 241 us -> none  [the longest x30 159 us: block_solve(): factor = jnp.linalg.cholesky(system)]
    pallas_call x0 -> x4, Pallas kernels: none -> 105 us  [the longest x1 48.9 us: solve(): pl.pallas_call(functools.partial(solve_kernel, step_size), out_shape=(jax...]
    dot_general x8 -> x0, matrix products: 30.4 us -> none  [the longest x4 14.8 us: kernel_slab(): jnp.einsum('rf,bf->rb', left_rows, right_rows, preferred_element_type=jnp...]
    another operation x40 -> x0, matrix products: 28.5 us -> none  [the longest x12 10.9 us: block_solve(): factor = jnp.linalg.cholesky(system)]
    another operation x35 -> x0, local copies, waits for them, and re-layouts: 22.7 us -> none  [the longest x27 22.4 us: block_solve(): lax.linalg.triangular_solve(factor, half_way, left_side=True, lower=True,...]
  transfers between devices with their start and end apart: 3 -> 0, of which waited for: 3 -> 0; matrix products, arithmetic and copies ran while one was open for 21% -> 0% of each run, Pallas kernels for 0% -> 0%
where the time goes in v2:
time: 113 us; the launch traced here: 112 us
  Pallas kernels  105 us (93%)
  local copies, waits for them, and re-layouts  6.71 us (6%)
    pallas_call x1, Pallas kernels, solve(): pl.pallas_call(functools.partial(solve_kernel, step_size), out_shape=(jax...  48.9 us
    pallas_call x1, Pallas kernels, fetch_blocks(): pl.pallas_call(fetch_kernel, out_shape=jax.ShapeDtypeStruct(shape, BF16),...  40 us
    pallas_call x1, Pallas kernels, slab_parts(): pl.pallas_call(slab_kernel, grid=(rows // CHUNK,), out_shape=(jax.ShapeDt...  11.2 us
    unnamed x16, local copies, waits for them, and re-layouts  6.71 us
    pallas_call x1, Pallas kernels, final(): pl.pallas_call(final_kernel, grid=(rows // ROWS_STEP,), out_shape=(jax.Sh...  4.76 us

profile of v2, /device:TPU:1, one launch (start us, length us, event | category | flops | bytes accessed | tf_op | source)
XLA Modules:
  0.0 112.3 jit_solution(12327081729222301943)
XLA Ops:
  0.6 0.0 copy-start
  0.6 2.2 %copy-done = bf16[4096,512]{1,0:T(8,128)(2,1)S(1)} copy-done((bf16[4096,512]{1,0:T(8,128)(2,1)S(1)}, bf16[4096,512]{1,0:T(8,128)(2,1)}, u32[]{:S(2)}) %copy-start) | copy-done | bytes 4194328
  2.8 0.0 copy-start.4
  2.8 0.7 copy-done.4
  3.5 0.0 copy-start.6
  3.5 0.7 copy-done.6
  4.2 0.0 copy-start.1
  4.2 40.0 %fetch_blocks.1 = bf16[2,16,32,512]{3,2,1,0:T(8,128)(2,1)S(1)} custom-call(s32[2]{0:T(128)S(1)} %copy-done.6, s32[2,4]{1,0:T(2,128)S(1)} %copy-done.4, bf16[32,128,512]{2,1,0:T(8,128)(2,1)S(1)} %bitcast.3), custom_call_target="tpu_custom_call" | custom-call | tf_op jit(solution)/shard_map/fetch_blocks/pallas_call | solution.py:262
  44.2 0.0 copy-done.1
  44.2 0.0 copy-start.2
  44.2 1.6 %copy-done.2 = f32[4096,128]{1,0:T(8,128)S(1)} copy-done((f32[4096,128]{1,0:T(8,128)S(1)}, f32[4096,128]{1,0:T(8,128)}, u32[]{:S(2)}) %copy-start.2) | copy-done | bytes 2097176
  45.8 0.0 copy-start.3
  45.8 1.6 %copy-done.3 = f32[4096,128]{1,0:T(8,128)S(1)} copy-done((f32[4096,128]{1,0:T(8,128)S(1)}, f32[4096,128]{1,0:T(8,128)}, u32[]{:S(2)}) %copy-start.3) | copy-done | bytes 2097176
  47.4 11.2 %slab_parts.1 = (bf16[1024,4096]{1,0:T(8,128)(2,1)S(1)}, f32[512,768]{1,0:T(8,128)S(1)}) custom-call(bf16[1024,512]{1,0:T(8,128)(2,1)S(1)} %bitcast.4, bf16[4096,512]{1,0:T(8,128)(2,1)S(1)} %copy-done.1, f32[4096,128]{1,0:T(8,128)S(1)} %copy-done.2, f32[4096,128]{1,0:T(8,128)S(1)} %copy-done.3), custom_call_target="tpu_custom_call" | custom-call | tf_op jit(solution)/shard_map/slab_parts/pallas_call | solution.py:314
  58.6 0.0 copy-start.5
  58.6 0.0 copy-start.7
  58.6 48.9 %solve.1 = (f32[1024,128]{1,0:T(8,128)S(1)}, bf16[128,1024]{1,0:T(8,128)(2,1)S(1)}) custom-call(bf16[1024,512]{1,0:T(8,128)(2,1)S(1)} %bitcast.5, f32[2,16,16,768]{3,2,1,0:T(8,128)S(1)} %bitcast.6), custom_call_target="tpu_custom_call" | custom-call | tf_op jit(solution)/shard_map/solve/pallas_call | solution.py:464
  107.5 0.0 copy-done.5
  107.5 0.0 copy-done.7
  107.5 4.8 %final.1 = (f32[4096,128]{1,0:T(8,128)}, f32[4096,128]{1,0:T(8,128)}) custom-call(s32[2]{0:T(128)S(1)} %copy-done.7, s32[2,4]{1,0:T(2,128)S(1)} %copy-done.5, f32[1024,128]{1,0:T(8,128)S(1)} %get-tuple-element.7.update_ref, bf16[128,1024]{1,0:T(8,128)(2,1)S(1)} %get-tuple-element.8.low_ref, bf16[1024,4096]{1,0:T(8,128)(2,1)S(1)} %get-tuple-element.9.slab_ref, ...), custom_call_target="tpu_custom_call" | custom-call | tf_op jit(solution)/shard_map/final/pallas_call | solution.py:512
Async XLA Ops:
  0.6 2.2 %copy-start = (bf16[4096,512]{1,0:T(8,128)(2,1)S(1)}, bf16[4096,512]{1,0:T(8,128)(2,1)}, u32[]{:S(2)}) copy-start(bf16[4096,512]{1,0:T(8,128)(2,1)} %feat_ref.1) | copy-start | bytes 12582916
  2.8 0.7 copy-start.4
  3.5 0.7 copy-start.6
  4.2 40.0 %copy-start.1 = (bf16[4096,512]{1,0:T(8,128)(2,1)S(1)}, bf16[4096,512]{1,0:T(8,128)(2,1)}, u32[]{:S(2)}) copy-start(bf16[4096,512]{1,0:T(8,128)(2,1)} %feat_ref.1) | copy-start | bytes 12582916
  44.2 1.6 %copy-start.2 = (f32[4096,128]{1,0:T(8,128)S(1)}, f32[4096,128]{1,0:T(8,128)}, u32[]{:S(2)}) copy-start(f32[4096,128]{1,0:T(8,128)} %res_ref.3) | copy-start | bytes 6291460
  45.8 1.6 %copy-start.3 = (f32[4096,128]{1,0:T(8,128)S(1)}, f32[4096,128]{1,0:T(8,128)}, u32[]{:S(2)}) copy-start(f32[4096,128]{1,0:T(8,128)} %coef_ref.3) | copy-start | bytes 6291460
  58.6 48.9 %copy-start.5 = (s32[2,4]{1,0:T(2,128)S(1)}, s32[2,4]{1,0:T(2,128)}, u32[]{:S(2)}) copy-start(s32[2,4]{1,0:T(2,128)} %tiles_ref.3) | copy-start | bytes 100
  58.6 48.9 %copy-start.7 = (s32[2]{0:T(128)S(1)}, s32[2]{0:T(128)}, u32[]{:S(2)}) copy-start(s32[2]{0:T(128)} %owner_ref.3) | copy-start | bytes 28

commit v3 on v0

v3 whole, which is shorter than its diff:
```python
import functools
import math

import jax
import jax.numpy as jnp
from jax import lax
from jax.experimental import pallas as pl
from jax.experimental.pallas import tpu as pltpu
from jax.sharding import PartitionSpec as P

MESH = pl.DeviceIdType.MESH
HI = lax.Precision.HIGHEST
F32 = jnp.float32
BF16 = jnp.bfloat16

BLOCK = 512
TILE = 128
STEPS = 2
RIDGE = 0.5
WIDTH = 512
TARGETS = 128
NX, NY, NZ = 4, 4, 8
NQ = NX * NY
CHUNK = 1024
ROWS_DEV = 4096
VMEM_BYTES = 64 << 20


def vmem():
    return pl.BlockSpec(memory_space=pltpu.VMEM)


def smem():
    return pl.BlockSpec(memory_space=pltpu.SMEM)


def dot(a, b, precision=None):
    return jnp.dot(a, b, precision=precision, preferred_element_type=F32)


def dot_nt(a, b, precision=None):
    return lax.dot_general(
        a, b, (((1,), (1,)), ((), ())), precision=precision, preferred_element_type=F32
    )


def place():
    across, within = lax.axis_index("rows"), lax.axis_index("sub")
    core = lax.rem(across, 2)
    y = lax.rem(lax.div(across, 2), NY)
    z = lax.div(across, 2 * NY) * 2 + lax.rem(within, 2)
    x = lax.div(within, 2)
    return (x, y, z), core


def device(chip, core):
    x, y, z = chip
    return (lax.div(z, 2) * (2 * NY) + y * 2 + core, x * 2 + lax.rem(z, 2))


SIZES = (NX, NY, NZ)


def moved(chip, step):
    return tuple(
        lax.rem(c + (s + size) % size, size) if s % size else c
        for c, s, size in zip(chip, step, SIZES)
    )


def back(step):
    return tuple(-s for s in step)


def hops(step):
    return sum(min(s, size - s) for s, size in zip(step, SIZES))


class Columns:
    size = NX * NY
    steps = sorted(
        [(i, j, 0) for i in range(NX) for j in range(NY) if i or j], key=lambda s: -hops(s)
    )

    @staticmethod
    def number(chip):
        return chip[0] * NY + chip[1]


class Planes:
    size = NZ
    steps = sorted([(0, 0, k) for k in range(1, NZ)], key=lambda s: -hops(s))

    @staticmethod
    def number(chip):
        return chip[2]


def greet(chip, core):
    barrier = pltpu.get_barrier_semaphore()
    others = [(moved(chip, step), core) for step in Columns.steps + Planes.steps]
    others.append((chip, 1 - core))
    for there, side in others:
        pl.semaphore_signal(barrier, inc=1, device_id=device(there, side), device_id_type=MESH)


def await_greetings():
    pl.semaphore_wait(pltpu.get_barrier_semaphore(), len(Columns.steps) + len(Planes.steps) + 1)


def remote(source, target, sems, i, where):
    return pltpu.make_async_remote_copy(
        src_ref=source,
        dst_ref=target,
        send_sem=sems.at[0, i],
        recv_sem=sems.at[1, i],
        device_id=device(*where),
        device_id_type=MESH,
    )


class Flow:
    def __init__(self, chip, core, first, second, part_at, total_at, scratch):
        self.chip, self.core, self.first, self.second = chip, core, first, second
        self.part_at, self.total_at = part_at, total_at
        self.recv_a, self.half, self.recv_b, self.recv_c = scratch[:4]
        self.sem_a, self.sem_b, self.sem_c, self.sem_e, self.sem_f = scratch[4:]
        self.steps = first.steps + [(0, 0, 0)]
        self.last = len(first.steps)
        self.mate = (chip, 1 - core)
        self.chunk = first.number(chip)
        self.slot = second.number(chip)

    def ahead(self, i):
        there = moved(self.chip, self.steps[i])
        return (there, self.core), self.first.number(there)

    def behind(self, i):
        return self.first.number(moved(self.chip, back(self.steps[i])))

    def a_copy(self, i):
        part = self.part_at(1 - self.core, self.ahead(i)[1])
        return remote(part, self.recv_a.at[i], self.sem_a, i, self.mate)

    def b_copy(self, i):
        return remote(self.half.at[i], self.recv_b.at[i], self.sem_b, i, self.ahead(i)[0])

    def c_copy(self, i, slot):
        there = moved(self.chip, self.second.steps[i])
        mine, target = self.recv_c.at[self.slot], self.recv_c.at[slot]
        return remote(mine, target, self.sem_c, i, (there, self.core))

    def e_copy(self, i, chunk):
        mine, target = self.total_at(self.core, self.chunk), self.total_at(self.core, chunk)
        return remote(mine, target, self.sem_e, i, self.ahead(i)[0])

    def f_copy(self, i, side):
        chunk = self.behind(i)
        mine, target = self.total_at(self.core, chunk), self.total_at(side, chunk)
        return remote(mine, target, self.sem_f, i, self.mate)

    def start_a(self, i):
        self.a_copy(i).start()

    def a_to_b(self, i):
        self.a_copy(i).wait_recv()
        self.half[i] = self.part_at(self.core, self.ahead(i)[1])[...] + self.recv_a[i]
        if i < self.last:
            self.b_copy(i).start()

    def b_to_c(self):
        chunk = self.half[self.last]
        for i in reversed(range(self.last)):
            self.b_copy(i).wait_recv()
            chunk = chunk + self.recv_b[i]
        self.recv_c[self.slot] = chunk
        for i in range(len(self.second.steps)):
            self.c_copy(i, self.slot).start()

    def c_to_e(self):
        for i in range(len(self.second.steps)):
            source = moved(self.chip, back(self.second.steps[i]))
            self.c_copy(i, self.second.number(source)).wait_recv()
        chunk = self.recv_c[0]
        for i in range(1, self.second.size):
            chunk = chunk + self.recv_c[i]
        self.total_at(self.core, self.chunk)[...] = chunk
        for i in range(self.last):
            self.e_copy(i, self.chunk).start()
        self.f_copy(self.last, self.core).start()

    def e_to_f(self, i):
        self.e_copy(i, self.behind(i)).wait_recv()
        self.f_copy(i, self.core).start()

    def finish(self):
        for i in reversed(range(self.first.size)):
            self.f_copy(i, 1 - self.core).wait_recv()

    def drain(self):
        for i in range(self.first.size):
            self.a_copy(i).wait_send()
            self.f_copy(i, self.core).wait_send()
        for i in range(self.last):
            self.b_copy(i).wait_send()
            self.e_copy(i, self.chunk).wait_send()
        for i in range(len(self.second.steps)):
            self.c_copy(i, self.slot).wait_send()


def flow_scratch(first, second, shape, dtype):
    def pair(n):
        return pltpu.SemaphoreType.DMA((2, n))

    n1, n2 = len(first.steps), len(second.steps)
    return [
        pltpu.VMEM((first.size, *shape), dtype),
        pltpu.VMEM((first.size, *shape), dtype),
        pltpu.VMEM((n1, *shape), dtype),
        pltpu.VMEM((second.size, *shape), dtype),
        pair(first.size),
        pair(n1),
        pair(n2),
        pair(n1),
        pair(first.size),
    ]


FLOW_SCRATCH = 9


class Flows:
    def __init__(self, *flows):
        self.flows = flows

    def in_turn(self, count, call):
        most = max(count(flow) for flow in self.flows)
        for i in range(most):
            for flow in self.flows:
                if i < count(flow):
                    call(flow, i)

    def start_a(self):
        self.in_turn(lambda f: f.first.size, lambda f, i: f.start_a(i))

    def a_to_b(self):
        self.in_turn(lambda f: f.first.size, lambda f, i: f.a_to_b(i))

    def b_to_c(self):
        for flow in reversed(self.flows):
            flow.b_to_c()

    def c_to_e(self):
        for flow in self.flows:
            flow.c_to_e()

    def e_to_f(self):
        self.in_turn(lambda f: f.last, lambda f, i: f.e_to_f(f.last - 1 - i))

    def finish(self):
        for flow in self.flows:
            flow.finish()

    def drain(self):
        for flow in self.flows:
            flow.drain()


PANEL = 4
HALF_TILE = TILE // 2


def eliminate(a, begin, end):
    n = TILE
    row = lax.broadcasted_iota(jnp.int32, (n, n), 0)
    lane = lax.broadcasted_iota(jnp.int32, (n, n), 1)
    for first in range(begin, end, PANEL):
        columns = [
            jnp.broadcast_to(a[:, first + j : first + j + 1], (n, n)) for j in range(PANEL)
        ]
        for j in range(PANEL):
            k = first + j
            column = columns[j]
            inverse = 1.0 / column[k : k + 1, :]
            column = jnp.where(row == k, column - 1.0, column)
            a = jnp.where(lane == k, jnp.where(row == k, 1.0, 0.0), a)
            a = a - column * (a[k : k + 1, :] * inverse)
            for jj in range(j + 1, PANEL):
                other = columns[jj]
                columns[jj] = other - column * (other[k : k + 1, :] * inverse)
    return a


def split3(wide):
    high = wide.astype(BF16)
    rest = wide - high.astype(F32)
    middle = rest.astype(BF16)
    low = (rest - middle.astype(F32)).astype(BF16)
    return high, middle, low


def product(left, right):
    lh, lm, ll = left
    rh, rm, rl = right
    small = dot(lh, rl) + dot(lm, rm) + dot(ll, rh)
    return dot(lh, rh) + (dot(lh, rm) + dot(lm, rh) + small)


LOG2E_SCALED = math.log2(math.e) / WIDTH


def column_norms(rows):
    wide = rows.astype(F32)
    return jnp.sum(wide * wide, axis=1, keepdims=True) * LOG2E_SCALED


def along_lanes(column):
    return jnp.transpose(jnp.broadcast_to(column, (column.shape[0], 128)))[0:1, :]


def kernel_of(cross, column, lane_row):
    return jnp.exp2((2.0 * LOG2E_SCALED) * cross - lane_row - column)


FETCH_ROWS = BLOCK // NQ
FETCH_CUT = 384
FETCH_FLOWS = ((Columns, Planes, (FETCH_ROWS, FETCH_CUT)), (Planes, Columns, (2, FETCH_ROWS, WIDTH - FETCH_CUT)))
HALF = BLOCK // 2
SUM_FLOWS = ((Columns, Planes, (HALF // NQ, BLOCK)), (Planes, Columns, (HALF // NZ, STEPS * TARGETS)))
CHUNKS = ROWS_DEV // CHUNK
CHUNK_TILES = CHUNK // TILE


def update_kernel(
    step_size,
    owner_ref,
    tiles_ref,
    feat_hbm,
    res_hbm,
    coef_hbm,
    update_ref,
    low_ref,
    slab_hbm,
    feat_ref,
    res_ref,
    coef_ref,
    weighted_ref,
    along_ref,
    slab_ref,
    load_sem,
    slab_sem,
    masked,
    blocks,
    norm_ref,
    product_part,
    product_sum,
    grad_part,
    grad_sum,
    inv,
    thirds,
    between,
    swap_sem,
    *scratch,
):
    loads = [
        pltpu.make_async_copy(source, target, load_sem.at[i])
        for i, (source, target) in enumerate(
            [(feat_hbm, feat_ref), (res_hbm, res_ref), (coef_hbm, coef_ref)]
        )
    ]
    loads[0].start()
    chip, core = place()
    greet(chip, core)
    for load in loads[1:]:
        load.start()

    me = lax.axis_index("rows") * lax.axis_size("sub") + lax.axis_index("sub")
    loads[0].wait()
    per_tile = TILE // FETCH_ROWS

    def build(s):
        mine = jnp.full((FETCH_ROWS, WIDTH), (owner_ref[s] == me).astype(F32)).astype(BF16)
        for t in range(BLOCK // TILE):
            tile = feat_ref[tiles_ref[s, t]]
            for i in range(per_tile):
                at = slice(i * FETCH_ROWS, (i + 1) * FETCH_ROWS)
                masked[s, t * per_tile + i] = tile[at] * mine

    left, right = pl.ds(0, FETCH_CUT), pl.ds(FETCH_CUT, WIDTH - FETCH_CUT)

    def pair_of(ref):
        return (
            lambda side, chunk: ref.at[side, chunk, :, left],
            lambda side, chunk: ref.at[side, pl.ds(2 * chunk, 2), :, right],
        )

    def flows_of(kinds, parts, totals, scratch):
        flows = []
        for i, (first, second, _) in enumerate(kinds):
            mine = scratch[i * FLOW_SCRATCH : (i + 1) * FLOW_SCRATCH]
            flows.append(Flow(chip, core, first, second, parts[i], totals[i], mine))
        return Flows(*flows)

    fetch = flows_of(FETCH_FLOWS, pair_of(masked), pair_of(blocks), scratch)
    build(1 - core)
    await_greetings()
    fetch.start_a()
    build(core)
    fetch.a_to_b()

    def norms_of(i, carry):
        rows = feat_ref[pl.ds(i * CHUNK_TILES, CHUNK_TILES)].reshape(CHUNK, WIDTH)
        along_ref[i] = jnp.broadcast_to(along_lanes(column_norms(rows)), (8, CHUNK))
        return carry

    lax.fori_loop(0, CHUNKS, norms_of, 0)
    fetch.b_to_c()
    for load in loads[1:]:
        load.wait()
    weighted_ref[...] = (res_ref[...] - RIDGE * coef_ref[...]).astype(BF16)
    product_part[...] = jnp.zeros_like(product_part)
    grad_part[...] = jnp.zeros_like(grad_part)
    fetch.c_to_e()
    fetch.e_to_f()
    fetch.finish()

    for s in range(STEPS):
        norm = column_norms(blocks[s].reshape(BLOCK, WIDTH))
        norm_ref[s] = jnp.broadcast_to(norm, (BLOCK, 128))

    def slab_copy(i):
        return pltpu.make_async_copy(slab_ref.at[i], slab_hbm.at[i], slab_sem.at[i])

    def slab_step(i, carry):
        feat = feat_ref[pl.ds(i * CHUNK_TILES, CHUNK_TILES)].reshape(CHUNK, WIDTH)
        weighted = weighted_ref[pl.ds(pl.multiple_of(i * CHUNK, CHUNK), CHUNK), :]
        along = along_ref[i][0:1, :]
        slabs = []
        for s in range(STEPS):
            cross = dot_nt(blocks[s].reshape(BLOCK, WIDTH), feat)
            slab = kernel_of(cross, norm_ref[s][:, 0:1], along).astype(BF16)
            slab_ref[i, pl.ds(s * BLOCK, BLOCK), :] = slab
            slabs.append(slab)
            term = dot(slab, weighted).reshape(2, NZ, HALF // NZ, TARGETS)
            grad_part[:, :, :, pl.ds(s * TARGETS, TARGETS)] += term
        term = dot_nt(slabs[1], slabs[0])
        product_part[...] += term.reshape(product_part.shape)
        slab_copy(i).start()
        return carry

    lax.fori_loop(0, CHUNKS, slab_step, 0)

    sums = flows_of(
        SUM_FLOWS,
        (
            lambda side, chunk: product_part.at[side, chunk],
            lambda side, chunk: grad_part.at[side, chunk],
        ),
        (
            lambda side, chunk: product_sum.at[side, chunk],
            lambda side, chunk: grad_sum.at[side, chunk],
        ),
        scratch[2 * FLOW_SCRATCH :],
    )
    sums.start_a()

    def block_kernel(a, b):
        cross = dot_nt(blocks[a].reshape(BLOCK, WIDTH), blocks[b].reshape(BLOCK, WIDTH))
        return kernel_of(cross, norm_ref[a][:, 0:1], along_lanes(norm_ref[b][:, 0:1]))

    row = lax.broadcasted_iota(jnp.int32, (BLOCK, BLOCK), 0)
    lane = lax.broadcasted_iota(jnp.int32, (BLOCK, BLOCK), 1)
    inv[core] = block_kernel(core, core) + jnp.where(row == lane, RIDGE, 0.0)
    sums.a_to_b()
    between[...] = block_kernel(1, 0).astype(BF16)

    stages = {2: sums.b_to_c, 4: sums.c_to_e, 6: sums.e_to_f}

    def hook(k, half):
        for at, stage in stages.items():
            if at % 2 == half:
                pl.when(k == at // 2)(stage)

    def step(k, carry):
        at = pl.ds(pl.multiple_of(k * TILE, TILE), TILE)
        inv[core, at, at] = eliminate(inv[core, at, at], 0, HALF_TILE)
        hook(k, 0)
        tile = eliminate(inv[core, at, at], HALF_TILE, TILE)
        inside = lax.div(lax.broadcasted_iota(jnp.int32, (TILE, BLOCK), 1), TILE) == k
        lead = dot(tile, inv[core, at, :], HI)
        lead = jnp.where(inside, jnp.concatenate([tile] * (BLOCK // TILE), axis=1), lead)
        column = inv[core, :, at]
        inv[core, :, at] = jnp.zeros_like(column)
        inv[core] -= dot(column, lead, HI)
        inv[core, at, :] = lead
        hook(k, 1)
        return carry

    lax.fori_loop(0, BLOCK // TILE, step, 0)

    def swap(side):
        return remote(inv.at[core], inv.at[side], swap_sem, 0, (chip, 1 - core))

    swap(core).start()
    swap(1 - core).wait_recv()
    for s in range(STEPS):
        for i, third in enumerate(split3(inv[s])):
            thirds[s, i] = third
    sums.finish()

    both = [(thirds[s, 0], thirds[s, 1], thirds[s, 2]) for s in range(STEPS)]
    grads = grad_sum[...].reshape(BLOCK, STEPS * TARGETS)
    first = product(both[0], split3(grads[:, :TARGETS])) * step_size
    first_low = first.astype(BF16)
    slab_product = product_sum[...].reshape(BLOCK, BLOCK)
    shift = sum(dot(third, first_low) for third in split3(slab_product))
    past = sum(dot(between[...], third) for third in split3(first))
    gradient = grads[:, TARGETS:] - shift - RIDGE * past
    second = product(both[1], split3(gradient)) * step_size
    update_ref[0:BLOCK] = first
    update_ref[BLOCK:] = second
    low_ref[:, 0:BLOCK] = jnp.transpose(first).astype(BF16)
    low_ref[:, BLOCK:] = jnp.transpose(second).astype(BF16)

    swap(core).wait_send()
    fetch.drain()
    sums.drain()
    for i in range(CHUNKS):
        slab_copy(i).wait()


def updates_of(step_size, block_owner, block_tiles, features, residual, coefficients):
    anywhere = pl.BlockSpec(memory_space=pl.ANY)
    tiled = features.reshape(-1, TILE, WIDTH)
    slab_shape = (CHUNKS, STEPS * BLOCK, CHUNK)
    fetch_shape = (STEPS, NQ, FETCH_ROWS, WIDTH)
    product_shape = (2, NQ, HALF // NQ, BLOCK)
    grad_shape = (2, NZ, HALF // NZ, STEPS * TARGETS)
    flows = []
    for first, second, shape in FETCH_FLOWS:
        flows += flow_scratch(first, second, shape, BF16)
    for first, second, shape in SUM_FLOWS:
        flows += flow_scratch(first, second, shape, F32)
    return pl.pallas_call(
        functools.partial(update_kernel, step_size),
        out_shape=(
            jax.ShapeDtypeStruct((STEPS * BLOCK, TARGETS), F32),
            jax.ShapeDtypeStruct((TARGETS, STEPS * BLOCK), BF16),
            jax.ShapeDtypeStruct(slab_shape, BF16),
        ),
        in_specs=[smem(), smem(), anywhere, anywhere, anywhere],
        out_specs=(vmem(), vmem(), anywhere),
        scratch_shapes=[
            pltpu.VMEM(tiled.shape, BF16),
            pltpu.VMEM(residual.shape, F32),
            pltpu.VMEM(coefficients.shape, F32),
            pltpu.VMEM(residual.shape, BF16),
            pltpu.VMEM((CHUNKS, 8, CHUNK), F32),
            pltpu.VMEM(slab_shape, BF16),
            pltpu.SemaphoreType.DMA((3,)),
            pltpu.SemaphoreType.DMA((CHUNKS,)),
            pltpu.VMEM(fetch_shape, BF16),
            pltpu.VMEM(fetch_shape, BF16),
            pltpu.VMEM((STEPS, BLOCK, 128), F32),
            pltpu.VMEM(product_shape, F32),
            pltpu.VMEM(product_shape, F32),
            pltpu.VMEM(grad_shape, F32),
            pltpu.VMEM(grad_shape, F32),
            pltpu.VMEM((STEPS, BLOCK, BLOCK), F32),
            pltpu.VMEM((STEPS, 3, BLOCK, BLOCK), BF16),
            pltpu.VMEM((BLOCK, BLOCK), BF16),
            pltpu.SemaphoreType.DMA((2, 1)),
            *flows,
        ],
        compiler_params=pltpu.CompilerParams(
            collective_id=0, has_side_effects=True, vmem_limit_bytes=VMEM_BYTES
        ),
        name="updates",
    )(block_owner, block_tiles, tiled, residual, coefficients)


ROWS_STEP = CHUNK


def final_kernel(
    owner_ref, tiles_ref, update_ref, low_ref, slab_ref, res_ref, coef_ref, res_out, coef_out
):
    step = pl.program_id(0)
    res_out[...] = res_ref[...] - jnp.transpose(dot(low_ref[...], slab_ref[0]))
    coef_out[...] = coef_ref[...]
    me = lax.axis_index("rows") * lax.axis_size("sub") + lax.axis_index("sub")
    tiles_here = ROWS_STEP // TILE
    for s in range(STEPS):
        for t in range(BLOCK // TILE):
            tile = tiles_ref[s, t]

            @pl.when((owner_ref[s] == me) & (lax.div(tile, tiles_here) == step))
            def _():
                at = pl.ds(pl.multiple_of(lax.rem(tile, tiles_here) * TILE, TILE), TILE)
                coef_out[at, :] += update_ref[pl.ds(s * BLOCK + t * TILE, TILE), :]


def final(owner, tiles, updates, low, slabs, residual, coefficients):
    rows = residual.shape[0]
    whole = lambda i: (0, 0)
    chunk = pl.BlockSpec((ROWS_STEP, TARGETS), lambda i: (i, 0))
    return pl.pallas_call(
        final_kernel,
        grid=(rows // ROWS_STEP,),
        out_shape=(
            jax.ShapeDtypeStruct(residual.shape, F32),
            jax.ShapeDtypeStruct(coefficients.shape, F32),
        ),
        in_specs=[
            smem(),
            smem(),
            pl.BlockSpec(updates.shape, whole),
            pl.BlockSpec(low.shape, whole),
            pl.BlockSpec((1, STEPS * BLOCK, ROWS_STEP), lambda i: (i, 0, 0)),
            chunk,
            chunk,
        ],
        out_specs=(chunk, chunk),
        compiler_params=pltpu.CompilerParams(vmem_limit_bytes=VMEM_BYTES),
        name="final",
    )(owner, tiles, updates, low, slabs, residual, coefficients)


def local(features, residual, coefficients, block_owner, block_tiles):
    devices = lax.axis_size("rows") * lax.axis_size("sub")
    step_size = 1.0 / math.sqrt(features.shape[0] * devices)
    updates, low, slabs = updates_of(
        step_size, block_owner, block_tiles, features, residual, coefficients
    )
    return final(block_owner, block_tiles, updates, low, slabs, residual, coefficients)


def solution(mesh):
    in_specs = (
        P(("rows", "sub"), None),
        P(("rows", "sub"), None),
        P(("rows", "sub"), None),
        P(),
        P(),
    )
    out_specs = (P(("rows", "sub"), None), P(("rows", "sub"), None))
    return jax.shard_map(local, mesh=mesh, in_specs=in_specs, out_specs=out_specs, check_vma=False)
```

time: 938 us -> 95.8 us (0.10); the launches traced: 927 us -> 95.7 us
  waiting for transfers between devices: 555 us -> 0 us
  other arithmetic: 252 us -> 0 us
  Pallas kernels: 0 us -> 95 us
  matrix products: 58.9 us -> 0 us
  local copies, waits for them, and re-layouts: 39.3 us -> 0 us
  between operations: 21.1 us -> 0.64 us
    psum x3 -> x0, waiting for transfers between devices: 555 us -> none  [the longest x2 299 us: local(): gradient = lax.psum(local_term, ('rows', 'sub'))]
    another operation x35 -> x0, other arithmetic: 241 us -> none  [the longest x30 159 us: block_solve(): factor = jnp.linalg.cholesky(system)]
    pallas_call x0 -> x2, Pallas kernels: none -> 95 us  [the longest x1 86.9 us: updates_of(): pl.pallas_call(functools.partial(update_kernel, step_size), out_shape=(ja...]
    dot_general x8 -> x0, matrix products: 30.4 us -> none  [the longest x4 14.8 us: kernel_slab(): jnp.einsum('rf,bf->rb', left_rows, right_rows, preferred_element_type=jnp...]
    another operation x40 -> x0, matrix products: 28.5 us -> none  [the longest x12 10.9 us: block_solve(): factor = jnp.linalg.cholesky(system)]
    another operation x35 -> x0, local copies, waits for them, and re-layouts: 22.7 us -> none  [the longest x27 22.4 us: block_solve(): lax.linalg.triangular_solve(factor, half_way, left_side=True, lower=True,...]
  transfers between devices with their start and end apart: 3 -> 0, of which waited for: 3 -> 0; matrix products, arithmetic and copies ran while one was open for 21% -> 0% of each run, Pallas kernels for 0% -> 0%
where the time goes in v3:
time: 95.8 us; the launch traced here: 95.7 us
  Pallas kernels  95 us (99%)
    pallas_call x1, Pallas kernels, updates_of(): pl.pallas_call(functools.partial(update_kernel, step_size), out_shape=(ja...  86.9 us
    pallas_call x1, Pallas kernels, final(): pl.pallas_call(final_kernel, grid=(rows // ROWS_STEP,), out_shape=(jax.Sh...  8.08 us

profile of v3, /device:TPU:1, one launch (start us, length us, event | category | flops | bytes accessed | tf_op | source)
XLA Modules:
  0.0 95.7 jit_solution(7970820874411606613)
XLA Ops:
  0.6 86.9 %updates.1 = (f32[1024,128]{1,0:T(8,128)}, bf16[128,1024]{1,0:T(8,128)(2,1)}, bf16[4,1024,1024]{2,1,0:T(8,128)(2,1)}) custom-call(s32[2]{0:T(128)} %owner_ref.3, s32[2,4]{1,0:T(2,128)} %tiles_ref.3, bf16[32,128,512]{2,1,0:T(8,128)(2,1)} %bitcast.1, f32[4096,128]{1,0:T(8,128)} %res_ref.1, f32[4096,128]{1,0:T(8,128)} %coef_ref.1), custom_call_target="tpu_custom_call" | custom-call | tf_op jit(solution)/shard_map/updates/pallas_call | solution.py:544
  87.6 8.1 %final.1 = (f32[4096,128]{1,0:T(8,128)}, f32[4096,128]{1,0:T(8,128)}) custom-call(s32[2]{0:T(128)} %owner_ref.3, s32[2,4]{1,0:T(2,128)} %tiles_ref.3, f32[1024,128]{1,0:T(8,128)} %get-tuple-element.5.update_ref, bf16[128,1024]{1,0:T(8,128)(2,1)} %get-tuple-element.6.low_ref, bf16[4,1024,1024]{2,1,0:T(8,128)(2,1)} %get-tuple-element.7.slab_ref, ...), custom_call_target="tpu_custom_call" | custom-call | tf_op jit(solution)/shard_map/final/pallas_call | solution.py:607

commit v4 on v3

--- a/solution.py
+++ b/solution.py
@@ -266,29 +266,35 @@
             flow.drain()
 
 
-PANEL = 4
-HALF_TILE = TILE // 2
-
-
-def eliminate(a, begin, end):
-    n = TILE
-    row = lax.broadcasted_iota(jnp.int32, (n, n), 0)
-    lane = lax.broadcasted_iota(jnp.int32, (n, n), 1)
-    for first in range(begin, end, PANEL):
-        columns = [
-            jnp.broadcast_to(a[:, first + j : first + j + 1], (n, n)) for j in range(PANEL)
-        ]
-        for j in range(PANEL):
-            k = first + j
-            column = columns[j]
-            inverse = 1.0 / column[k : k + 1, :]
-            column = jnp.where(row == k, column - 1.0, column)
-            a = jnp.where(lane == k, jnp.where(row == k, 1.0, 0.0), a)
-            a = a - column * (a[k : k + 1, :] * inverse)
-            for jj in range(j + 1, PANEL):
-                other = columns[jj]
-                columns[jj] = other - column * (other[k : k + 1, :] * inverse)
-    return a
+PANEL = 16
+PANELS = TILE // PANEL
+
+
+def eliminate(a, panel):
+    n, first = TILE, panel * PANEL
+    mine = slice(first, first + PANEL)
+    row = lax.broadcasted_iota(jnp.int32, (PANEL, n), 0)
+    lane = lax.broadcasted_iota(jnp.int32, (PANEL, n), 1)
+    lane_all = lax.broadcasted_iota(jnp.int32, (n, n), 1)
+    columns = [jnp.broadcast_to(a[:, first + j : first + j + 1], (n, n)) for j in range(PANEL)]
+    square = [column[mine] for column in columns]
+    rows = jnp.where(
+        (lane >= first) & (lane < first + PANEL),
+        jnp.where(lane - first == row, 1.0, 0.0),
+        a[mine],
+    )
+    for k in range(PANEL):
+        inverse = 1.0 / square[k][k : k + 1]
+        column = jnp.where(row == k, square[k] - 1.0, square[k])
+        for j in range(k + 1, PANEL):
+            square[j] = square[j] - column * (square[j][k : k + 1] * inverse)
+        rows = rows - column * (rows[k : k + 1] * inverse)
+    change = columns[0] * rows[0:1]
+    for j in range(1, PANEL):
+        change = change + columns[j] * rows[j : j + 1]
+    a = jnp.where((lane_all >= first) & (lane_all < first + PANEL), 0.0, a) - change
+    pieces = [a[:first], rows, a[first + PANEL :]]
+    return jnp.concatenate([piece for piece in pieces if piece.shape[0]], axis=0)
 
 
 def split3(wide):
@@ -359,6 +365,7 @@
     inv,
     thirds,
     between,
+    first_tile,
     swap_sem,
     *scratch,
 ):
@@ -418,8 +425,6 @@
     for load in loads[1:]:
         load.wait()
     weighted_ref[...] = (res_ref[...] - RIDGE * coef_ref[...]).astype(BF16)
-    product_part[...] = jnp.zeros_like(product_part)
-    grad_part[...] = jnp.zeros_like(grad_part)
     fetch.c_to_e()
     fetch.e_to_f()
     fetch.finish()
@@ -429,26 +434,45 @@
         norm_ref[s] = jnp.broadcast_to(norm, (BLOCK, 128))
 
     def slab_copy(i):
-        return pltpu.make_async_copy(slab_ref.at[i], slab_hbm.at[i], slab_sem.at[i])
-
-    def slab_step(i, carry):
-        feat = feat_ref[pl.ds(i * CHUNK_TILES, CHUNK_TILES)].reshape(CHUNK, WIDTH)
-        weighted = weighted_ref[pl.ds(pl.multiple_of(i * CHUNK, CHUNK), CHUNK), :]
-        along = along_ref[i][0:1, :]
-        slabs = []
+        at = pl.ds(i * CHUNK, CHUNK)
+        return pltpu.make_async_copy(slab_ref.at[:, at], slab_hbm.at[:, at], slab_sem.at[i])
+
+    def block_rows(s):
+        return blocks[s].reshape(BLOCK, WIDTH)
+
+    def cross_of(unit):
+        i, s = unit // STEPS, unit % STEPS
+        feat = feat_ref[i * CHUNK_TILES : (i + 1) * CHUNK_TILES].reshape(CHUNK, WIDTH)
+        return dot_nt(block_rows(s), feat)
+
+    row = lax.broadcasted_iota(jnp.int32, (BLOCK, BLOCK), 0)
+    lane = lax.broadcasted_iota(jnp.int32, (BLOCK, BLOCK), 1)
+    ridge = jnp.where(row == lane, RIDGE, 0.0)
+    corner = blocks[core, 0 : TILE // FETCH_ROWS].reshape(TILE, WIDTH)
+    corner_norm = norm_ref[core, 0:TILE, 0:1]
+    tile = kernel_of(dot_nt(corner, corner), corner_norm, along_lanes(corner_norm))
+    tile = tile + ridge[:TILE, :TILE]
+    units = CHUNKS * STEPS
+    cross = cross_of(0)
+    for unit in range(units):
+        i, s = unit // STEPS, unit % STEPS
+        later = cross_of(unit + 1) if unit + 1 < units else None
+        slab = kernel_of(cross, norm_ref[s][:, 0:1], along_ref[i][0:1, :]).astype(BF16)
+        slab_ref[s * BLOCK : (s + 1) * BLOCK, i * CHUNK : (i + 1) * CHUNK] = slab
+        if unit < PANELS:
+            tile = eliminate(tile, unit)
+        if s == STEPS - 1:
+            slab_copy(i).start()
+        cross = later
+    first_tile[...] = tile
+
+    def share(half):
+        at = [pl.ds(pl.multiple_of(s * BLOCK + half * HALF, HALF), HALF) for s in range(STEPS)]
         for s in range(STEPS):
-            cross = dot_nt(blocks[s].reshape(BLOCK, WIDTH), feat)
-            slab = kernel_of(cross, norm_ref[s][:, 0:1], along).astype(BF16)
-            slab_ref[i, pl.ds(s * BLOCK, BLOCK), :] = slab
-            slabs.append(slab)
-            term = dot(slab, weighted).reshape(2, NZ, HALF // NZ, TARGETS)
-            grad_part[:, :, :, pl.ds(s * TARGETS, TARGETS)] += term
-        term = dot_nt(slabs[1], slabs[0])
-        product_part[...] += term.reshape(product_part.shape)
-        slab_copy(i).start()
-        return carry
-
-    lax.fori_loop(0, CHUNKS, slab_step, 0)
+            term = dot(slab_ref[at[s], :], weighted_ref[...]).reshape(NZ, HALF // NZ, TARGETS)
+            grad_part[half, :, :, s * TARGETS : (s + 1) * TARGETS] = term
+        term = dot_nt(slab_ref[at[1], :], slab_ref[0:BLOCK, :])
+        product_part[half] = term.reshape(product_part.shape[1:])
 
     sums = flows_of(
         SUM_FLOWS,
@@ -462,30 +486,20 @@
         ),
         scratch[2 * FLOW_SCRATCH :],
     )
+    share(1 - core)
     sums.start_a()
+    share(core)
+    sums.a_to_b()
 
     def block_kernel(a, b):
-        cross = dot_nt(blocks[a].reshape(BLOCK, WIDTH), blocks[b].reshape(BLOCK, WIDTH))
+        cross = dot_nt(block_rows(a), block_rows(b))
         return kernel_of(cross, norm_ref[a][:, 0:1], along_lanes(norm_ref[b][:, 0:1]))
 
-    row = lax.broadcasted_iota(jnp.int32, (BLOCK, BLOCK), 0)
-    lane = lax.broadcasted_iota(jnp.int32, (BLOCK, BLOCK), 1)
-    inv[core] = block_kernel(core, core) + jnp.where(row == lane, RIDGE, 0.0)
-    sums.a_to_b()
+    inv[core] = block_kernel(core, core) + ridge
     between[...] = block_kernel(1, 0).astype(BF16)
 
-    stages = {2: sums.b_to_c, 4: sums.c_to_e, 6: sums.e_to_f}
-
-    def hook(k, half):
-        for at, stage in stages.items():
-            if at % 2 == half:
-                pl.when(k == at // 2)(stage)
-
-    def step(k, carry):
+    def spread(k, tile):
         at = pl.ds(pl.multiple_of(k * TILE, TILE), TILE)
-        inv[core, at, at] = eliminate(inv[core, at, at], 0, HALF_TILE)
-        hook(k, 0)
-        tile = eliminate(inv[core, at, at], HALF_TILE, TILE)
         inside = lax.div(lax.broadcasted_iota(jnp.int32, (TILE, BLOCK), 1), TILE) == k
         lead = dot(tile, inv[core, at, :], HI)
         lead = jnp.where(inside, jnp.concatenate([tile] * (BLOCK // TILE), axis=1), lead)
@@ -493,10 +507,24 @@
         inv[core, :, at] = jnp.zeros_like(column)
         inv[core] -= dot(column, lead, HI)
         inv[core, at, :] = lead
-        hook(k, 1)
+
+    stages = {(1, 2): sums.b_to_c, (2, 2): sums.c_to_e, (3, 2): sums.e_to_f}
+
+    def step(k, carry):
+        at = pl.ds(pl.multiple_of(k * TILE, TILE), TILE)
+        for part in range(4):
+            tile = inv[core, at, at]
+            for panel in range(part * PANELS // 4, (part + 1) * PANELS // 4):
+                tile = eliminate(tile, panel)
+            inv[core, at, at] = tile
+            for (at_k, at_part), stage in stages.items():
+                if at_part == part:
+                    pl.when(k == at_k)(stage)
+        spread(k, inv[core, at, at])
         return carry
 
-    lax.fori_loop(0, BLOCK // TILE, step, 0)
+    spread(0, first_tile[...])
+    lax.fori_loop(1, BLOCK // TILE, step, 0)
 
     def swap(side):
         return remote(inv.at[core], inv.at[side], swap_sem, 0, (chip, 1 - core))
@@ -531,8 +559,9 @@
 
 def updates_of(step_size, block_owner, block_tiles, features, residual, coefficients):
     anywhere = pl.BlockSpec(memory_space=pl.ANY)
+    hbm = pl.BlockSpec(memory_space=pltpu.HBM)
     tiled = features.reshape(-1, TILE, WIDTH)
-    slab_shape = (CHUNKS, STEPS * BLOCK, CHUNK)
+    slab_shape = (STEPS * BLOCK, ROWS_DEV)
     fetch_shape = (STEPS, NQ, FETCH_ROWS, WIDTH)
     product_shape = (2, NQ, HALF // NQ, BLOCK)
     grad_shape = (2, NZ, HALF // NZ, STEPS * TARGETS)
@@ -546,9 +575,9 @@
         out_shape=(
             jax.ShapeDtypeStruct((STEPS * BLOCK, TARGETS), F32),
             jax.ShapeDtypeStruct((TARGETS, STEPS * BLOCK), BF16),
-            jax.ShapeDtypeStruct(slab_shape, BF16),
+            pltpu.VMEM(slab_shape, BF16),
         ),
-        in_specs=[smem(), smem(), anywhere, anywhere, anywhere],
+        in_specs=[smem(), smem(), hbm, hbm, hbm],
         out_specs=(vmem(), vmem(), anywhere),
         scratch_shapes=[
             pltpu.VMEM(tiled.shape, BF16),
@@ -569,11 +598,12 @@
             pltpu.VMEM((STEPS, BLOCK, BLOCK), F32),
             pltpu.VMEM((STEPS, 3, BLOCK, BLOCK), BF16),
             pltpu.VMEM((BLOCK, BLOCK), BF16),
+            pltpu.VMEM((TILE, TILE), F32),
             pltpu.SemaphoreType.DMA((2, 1)),
             *flows,
         ],
         compiler_params=pltpu.CompilerParams(
-            collective_id=0, has_side_effects=True, vmem_limit_bytes=VMEM_BYTES
+            collective_id=0, has_side_effects=True, vmem_limit_bytes=44 << 20
         ),
         name="updates",
     )(block_owner, block_tiles, tiled, residual, coefficients)
@@ -586,7 +616,7 @@
     owner_ref, tiles_ref, update_ref, low_ref, slab_ref, res_ref, coef_ref, res_out, coef_out
 ):
     step = pl.program_id(0)
-    res_out[...] = res_ref[...] - jnp.transpose(dot(low_ref[...], slab_ref[0]))
+    res_out[...] = res_ref[...] - jnp.transpose(dot(low_ref[...], slab_ref[...]))
     coef_out[...] = coef_ref[...]
     me = lax.axis_index("rows") * lax.axis_size("sub") + lax.axis_index("sub")
     tiles_here = ROWS_STEP // TILE
@@ -616,12 +646,12 @@
             smem(),
             pl.BlockSpec(updates.shape, whole),
             pl.BlockSpec(low.shape, whole),
-            pl.BlockSpec((1, STEPS * BLOCK, ROWS_STEP), lambda i: (i, 0, 0)),
+            pl.BlockSpec((STEPS * BLOCK, ROWS_STEP), lambda i: (0, i)),
             chunk,
             chunk,
         ],
         out_specs=(chunk, chunk),
-        compiler_params=pltpu.CompilerParams(vmem_limit_bytes=VMEM_BYTES),
+        compiler_params=pltpu.CompilerParams(vmem_limit_bytes=24 << 20),
         name="final",
     )(owner, tiles, updates, low, slabs, residual, coefficients)
 

time: 95.8 us -> 93.1 us (0.972)
  Pallas kernels: 95 us -> 91 us
  local copies, waits for them, and re-layouts: 0 us -> 1.33 us
    pallas_call x1, Pallas kernels: 8.08 us -> 4.75 us  [final(): pl.pallas_call(final_kernel, grid=(rows // ROWS_STEP,), out_shape=(jax.Sh...]
    unnamed x0 -> x8, local copies, waits for them, and re-layouts: none -> 1.33 us
where the time goes in v4:
time: 93.1 us; the launch traced here: 93 us
  Pallas kernels  91 us (98%)
  local copies, waits for them, and re-layouts  1.33 us (1%)
    pallas_call x1, Pallas kernels, updates_of(): pl.pallas_call(functools.partial(update_kernel, step_size), out_shape=(ja...  86.2 us
    pallas_call x1, Pallas kernels, final(): pl.pallas_call(final_kernel, grid=(rows // ROWS_STEP,), out_shape=(jax.Sh...  4.75 us

profile of v4, /device:TPU:1, one launch (start us, length us, event | category | flops | bytes accessed | tf_op | source)
XLA Modules:
  0.0 93.0 jit_solution(2753561615913013768)
XLA Ops:
  0.6 0.0 copy-start.2
  0.6 0.7 copy-done.2
  1.3 0.0 copy-start.3
  1.3 0.7 copy-done.3
  2.0 0.0 copy-start
  2.0 0.0 copy-start.1
  2.0 86.2 %updates.1 = (f32[1024,128]{1,0:T(8,128)S(1)}, bf16[128,1024]{1,0:T(8,128)(2,1)S(1)}, bf16[1024,4096]{1,0:T(8,128)(2,1)S(1)}) custom-call(s32[2]{0:T(128)S(1)} %copy-done.3, s32[2,4]{1,0:T(2,128)S(1)} %copy-done.2, bf16[32,128,512]{2,1,0:T(8,128)(2,1)} %bitcast.1, f32[4096,128]{1,0:T(8,128)} %res_ref.1, f32[4096,128]{1,0:T(8,128)} %coef_ref.1), custom_call_target="tpu_custom_call" | custom-call | tf_op jit(solution)/shard_map/updates/pallas_call | solution.py:573
  88.2 0.0 copy-done
  88.2 0.0 copy-done.1
  88.2 4.8 %final.1 = (f32[4096,128]{1,0:T(8,128)}, f32[4096,128]{1,0:T(8,128)}) custom-call(s32[2]{0:T(128)S(1)} %copy-done.3, s32[2,4]{1,0:T(2,128)S(1)} %copy-done.2, f32[1024,128]{1,0:T(8,128)S(1)} %get-tuple-element.5.update_ref, bf16[128,1024]{1,0:T(8,128)(2,1)S(1)} %get-tuple-element.6.low_ref, bf16[1024,4096]{1,0:T(8,128)(2,1)S(1)} %get-tuple-element.7.slab_ref, ...), custom_call_target="tpu_custom_call" | custom-call | tf_op jit(solution)/shard_map/final/pallas_call | solution.py:637
Async XLA Ops:
  0.6 0.7 copy-start.2
  1.3 0.7 copy-start.3
  2.0 86.2 %copy-start = (f32[4096,128]{1,0:T(8,128)S(1)}, f32[4096,128]{1,0:T(8,128)}, u32[]{:S(2)}) copy-start(f32[4096,128]{1,0:T(8,128)} %res_ref.1) | copy-start | bytes 6291460
  2.0 86.2 %copy-start.1 = (f32[4096,128]{1,0:T(8,128)S(1)}, f32[4096,128]{1,0:T(8,128)}, u32[]{:S(2)}) copy-start(f32[4096,128]{1,0:T(8,128)} %coef_ref.1) | copy-start | bytes 6291460

commit v5 on v4

--- a/solution.py
+++ b/solution.py
@@ -305,11 +305,17 @@
     return high, middle, low
 
 
+def stacked_dot(thirds, right):
+    rows = thirds[0].shape[0]
+    whole = dot(jnp.concatenate(thirds, axis=0), right)
+    return [whole[i * rows : (i + 1) * rows] for i in range(len(thirds))]
+
+
 def product(left, right):
-    lh, lm, ll = left
-    rh, rm, rl = right
-    small = dot(lh, rl) + dot(lm, rm) + dot(ll, rh)
-    return dot(lh, rh) + (dot(lh, rm) + dot(lm, rh) + small)
+    high = stacked_dot(left, right[0])
+    middle = stacked_dot(left[:2], right[1])
+    low = dot(left[0], right[2])
+    return high[0] + ((high[1] + middle[0]) + (high[2] + middle[1] + low))
 
 
 LOG2E_SCALED = math.log2(math.e) / WIDTH
@@ -346,15 +352,13 @@
     coef_hbm,
     update_ref,
     low_ref,
-    slab_hbm,
+    slab_ref,
     feat_ref,
     res_ref,
     coef_ref,
     weighted_ref,
     along_ref,
-    slab_ref,
     load_sem,
-    slab_sem,
     masked,
     blocks,
     norm_ref,
@@ -427,24 +431,22 @@
     weighted_ref[...] = (res_ref[...] - RIDGE * coef_ref[...]).astype(BF16)
     fetch.c_to_e()
     fetch.e_to_f()
-    fetch.finish()
-
-    for s in range(STEPS):
-        norm = column_norms(blocks[s].reshape(BLOCK, WIDTH))
-        norm_ref[s] = jnp.broadcast_to(norm, (BLOCK, 128))
-
-    def slab_copy(i):
-        at = pl.ds(i * CHUNK, CHUNK)
-        return pltpu.make_async_copy(slab_ref.at[:, at], slab_hbm.at[:, at], slab_sem.at[i])
 
     def block_rows(s):
         return blocks[s].reshape(BLOCK, WIDTH)
 
+    def set_norm(s):
+        norm_ref[s] = jnp.broadcast_to(column_norms(block_rows(s)), (BLOCK, 128))
+
+    sides = [core] * CHUNKS + [1 - core] * CHUNKS
+    units = len(sides)
+
     def cross_of(unit):
-        i, s = unit // STEPS, unit % STEPS
+        i = unit % CHUNKS
         feat = feat_ref[i * CHUNK_TILES : (i + 1) * CHUNK_TILES].reshape(CHUNK, WIDTH)
-        return dot_nt(block_rows(s), feat)
-
+        return dot_nt(block_rows(sides[unit]), feat)
+
+    set_norm(core)
     row = lax.broadcasted_iota(jnp.int32, (BLOCK, BLOCK), 0)
     lane = lax.broadcasted_iota(jnp.int32, (BLOCK, BLOCK), 1)
     ridge = jnp.where(row == lane, RIDGE, 0.0)
@@ -452,17 +454,18 @@
     corner_norm = norm_ref[core, 0:TILE, 0:1]
     tile = kernel_of(dot_nt(corner, corner), corner_norm, along_lanes(corner_norm))
     tile = tile + ridge[:TILE, :TILE]
-    units = CHUNKS * STEPS
     cross = cross_of(0)
     for unit in range(units):
-        i, s = unit // STEPS, unit % STEPS
+        i = unit % CHUNKS
+        if unit == CHUNKS - 1:
+            fetch.finish()
+            set_norm(1 - core)
         later = cross_of(unit + 1) if unit + 1 < units else None
-        slab = kernel_of(cross, norm_ref[s][:, 0:1], along_ref[i][0:1, :]).astype(BF16)
-        slab_ref[s * BLOCK : (s + 1) * BLOCK, i * CHUNK : (i + 1) * CHUNK] = slab
+        slab = kernel_of(cross, norm_ref[sides[unit]][:, 0:1], along_ref[i][0:1, :]).astype(BF16)
+        at = pl.ds(pl.multiple_of(sides[unit] * BLOCK, BLOCK), BLOCK)
+        slab_ref[at, i * CHUNK : (i + 1) * CHUNK] = slab
         if unit < PANELS:
             tile = eliminate(tile, unit)
-        if s == STEPS - 1:
-            slab_copy(i).start()
         cross = later
     first_tile[...] = tile
 
@@ -471,7 +474,7 @@
         for s in range(STEPS):
             term = dot(slab_ref[at[s], :], weighted_ref[...]).reshape(NZ, HALF // NZ, TARGETS)
             grad_part[half, :, :, s * TARGETS : (s + 1) * TARGETS] = term
-        term = dot_nt(slab_ref[at[1], :], slab_ref[0:BLOCK, :])
+        term = dot_nt(slab_ref[at[0], :], slab_ref[BLOCK:, :])
         product_part[half] = term.reshape(product_part.shape[1:])
 
     sums = flows_of(
@@ -496,7 +499,7 @@
         return kernel_of(cross, norm_ref[a][:, 0:1], along_lanes(norm_ref[b][:, 0:1]))
 
     inv[core] = block_kernel(core, core) + ridge
-    between[...] = block_kernel(1, 0).astype(BF16)
+    between[...] = block_kernel(0, 1).astype(BF16)
 
     def spread(k, tile):
         at = pl.ds(pl.multiple_of(k * TILE, TILE), TILE)
@@ -508,7 +511,7 @@
         inv[core] -= dot(column, lead, HI)
         inv[core, at, :] = lead
 
-    stages = {(1, 2): sums.b_to_c, (2, 2): sums.c_to_e, (3, 2): sums.e_to_f}
+    stages = {(1, 3): sums.b_to_c, (3, 0): sums.c_to_e}
 
     def step(k, carry):
         at = pl.ds(pl.multiple_of(k * TILE, TILE), TILE)
@@ -529,36 +532,36 @@
     def swap(side):
         return remote(inv.at[core], inv.at[side], swap_sem, 0, (chip, 1 - core))
 
-    swap(core).start()
-    swap(1 - core).wait_recv()
-    for s in range(STEPS):
+    def split(s):
         for i, third in enumerate(split3(inv[s])):
             thirds[s, i] = third
+
+    swap(core).start()
+    split(core)
+    swap(1 - core).wait_recv()
+    split(1 - core)
+    sums.e_to_f()
     sums.finish()
 
-    both = [(thirds[s, 0], thirds[s, 1], thirds[s, 2]) for s in range(STEPS)]
-    grads = grad_sum[...].reshape(BLOCK, STEPS * TARGETS)
-    first = product(both[0], split3(grads[:, :TARGETS])) * step_size
+    both = [[thirds[s, i] for i in range(3)] for s in range(STEPS)]
+    grads = jnp.transpose(grad_sum[...].reshape(BLOCK, STEPS * TARGETS))
+    first = product(split3(grads[:TARGETS]), both[0]) * step_size
     first_low = first.astype(BF16)
     slab_product = product_sum[...].reshape(BLOCK, BLOCK)
-    shift = sum(dot(third, first_low) for third in split3(slab_product))
-    past = sum(dot(between[...], third) for third in split3(first))
-    gradient = grads[:, TARGETS:] - shift - RIDGE * past
-    second = product(both[1], split3(gradient)) * step_size
-    update_ref[0:BLOCK] = first
-    update_ref[BLOCK:] = second
-    low_ref[:, 0:BLOCK] = jnp.transpose(first).astype(BF16)
-    low_ref[:, BLOCK:] = jnp.transpose(second).astype(BF16)
+    shift = sum(dot(first_low, third) for third in split3(slab_product))
+    past = sum(stacked_dot(split3(first), between[...]))
+    gradient = grads[TARGETS:] - shift - RIDGE * past
+    second = product(split3(gradient), both[1]) * step_size
+    for s, update in enumerate((first, second)):
+        update_ref[s] = update
+        low_ref[:, s * BLOCK : (s + 1) * BLOCK] = update.astype(BF16)
 
     swap(core).wait_send()
     fetch.drain()
     sums.drain()
-    for i in range(CHUNKS):
-        slab_copy(i).wait()
 
 
 def updates_of(step_size, block_owner, block_tiles, features, residual, coefficients):
-    anywhere = pl.BlockSpec(memory_space=pl.ANY)
     hbm = pl.BlockSpec(memory_space=pltpu.HBM)
     tiled = features.reshape(-1, TILE, WIDTH)
     slab_shape = (STEPS * BLOCK, ROWS_DEV)
@@ -573,21 +576,19 @@
     return pl.pallas_call(
         functools.partial(update_kernel, step_size),
         out_shape=(
-            jax.ShapeDtypeStruct((STEPS * BLOCK, TARGETS), F32),
-            jax.ShapeDtypeStruct((TARGETS, STEPS * BLOCK), BF16),
+            pltpu.VMEM((STEPS, TARGETS, BLOCK), F32),
+            pltpu.VMEM((TARGETS, STEPS * BLOCK), BF16),
             pltpu.VMEM(slab_shape, BF16),
         ),
         in_specs=[smem(), smem(), hbm, hbm, hbm],
-        out_specs=(vmem(), vmem(), anywhere),
+        out_specs=(vmem(), vmem(), vmem()),
         scratch_shapes=[
             pltpu.VMEM(tiled.shape, BF16),
             pltpu.VMEM(residual.shape, F32),
             pltpu.VMEM(coefficients.shape, F32),
             pltpu.VMEM(residual.shape, BF16),
             pltpu.VMEM((CHUNKS, 8, CHUNK), F32),
-            pltpu.VMEM(slab_shape, BF16),
             pltpu.SemaphoreType.DMA((3,)),
-            pltpu.SemaphoreType.DMA((CHUNKS,)),
             pltpu.VMEM(fetch_shape, BF16),
             pltpu.VMEM(fetch_shape, BF16),
             pltpu.VMEM((STEPS, BLOCK, 128), F32),
@@ -603,7 +604,7 @@
             *flows,
         ],
         compiler_params=pltpu.CompilerParams(
-            collective_id=0, has_side_effects=True, vmem_limit_bytes=44 << 20
+            collective_id=0, has_side_effects=True, vmem_limit_bytes=48 << 20
         ),
         name="updates",
     )(block_owner, block_tiles, tiled, residual, coefficients)
@@ -616,8 +617,9 @@
     owner_ref, tiles_ref, update_ref, low_ref, slab_ref, res_ref, coef_ref, res_out, coef_out
 ):
     step = pl.program_id(0)
-    res_out[...] = res_ref[...] - jnp.transpose(dot(low_ref[...], slab_ref[...]))
-    coef_out[...] = coef_ref[...]
+    here = pl.ds(pl.multiple_of(step * ROWS_STEP, ROWS_STEP), ROWS_STEP)
+    res_out[...] = res_ref[here, :] - jnp.transpose(dot(low_ref[...], slab_ref[:, here]))
+    coef_out[...] = coef_ref[here, :]
     me = lax.axis_index("rows") * lax.axis_size("sub") + lax.axis_index("sub")
     tiles_here = ROWS_STEP // TILE
     for s in range(STEPS):
@@ -627,12 +629,11 @@
             @pl.when((owner_ref[s] == me) & (lax.div(tile, tiles_here) == step))
             def _():
                 at = pl.ds(pl.multiple_of(lax.rem(tile, tiles_here) * TILE, TILE), TILE)
-                coef_out[at, :] += update_ref[pl.ds(s * BLOCK + t * TILE, TILE), :]
+                coef_out[at, :] += jnp.transpose(update_ref[s, :, t * TILE : (t + 1) * TILE])
 
 
 def final(owner, tiles, updates, low, slabs, residual, coefficients):
     rows = residual.shape[0]
-    whole = lambda i: (0, 0)
     chunk = pl.BlockSpec((ROWS_STEP, TARGETS), lambda i: (i, 0))
     return pl.pallas_call(
         final_kernel,
@@ -641,15 +642,7 @@
             jax.ShapeDtypeStruct(residual.shape, F32),
             jax.ShapeDtypeStruct(coefficients.shape, F32),
         ),
-        in_specs=[
-            smem(),
-            smem(),
-            pl.BlockSpec(updates.shape, whole),
-            pl.BlockSpec(low.shape, whole),
-            pl.BlockSpec((STEPS * BLOCK, ROWS_STEP), lambda i: (0, i)),
-            chunk,
-            chunk,
-        ],
+        in_specs=[smem(), smem(), vmem(), vmem(), vmem(), vmem(), vmem()],
         out_specs=(chunk, chunk),
         compiler_params=pltpu.CompilerParams(vmem_limit_bytes=24 << 20),
         name="final",

time: 93.1 us -> 80.8 us (0.87)
  Pallas kernels: 91 us -> 80 us
  local copies, waits for them, and re-layouts: 1.33 us -> 0.02 us
    pallas_call x1, Pallas kernels: 86.2 us -> 75.5 us  [updates_of(): pl.pallas_call(functools.partial(update_kernel, step_size), out_shape=(pl...]
    unnamed x8, local copies, waits for them, and re-layouts: 1.33 us -> 0.02 us
where the time goes in v5:
time: 80.8 us; the launch traced here: 80.7 us
  Pallas kernels  80 us (99%)
    pallas_call x1, Pallas kernels, updates_of(): pl.pallas_call(functools.partial(update_kernel, step_size), out_shape=(pl...  75.5 us
    pallas_call x1, Pallas kernels, final(): pl.pallas_call(final_kernel, grid=(rows // ROWS_STEP,), out_shape=(jax.Sh...  4.47 us

profile of v5, /device:TPU:1, one launch (start us, length us, event | category | flops | bytes accessed | tf_op | source)
XLA Modules:
  0.0 80.7 jit_solution(5231807533347874946)
XLA Ops:
  0.6 0.0 copy-start
  0.6 0.0 copy-start.1
  0.7 0.0 copy-start.2
  0.7 0.0 copy-start.3
  0.7 75.5 %updates.1 = (f32[2,128,512]{2,1,0:T(8,128)S(1)}, bf16[128,1024]{1,0:T(8,128)(2,1)S(1)}, bf16[1024,4096]{1,0:T(8,128)(2,1)S(1)}) custom-call(s32[2]{0:T(128)} %owner_ref.3, s32[2,4]{1,0:T(2,128)} %tiles_ref.3, bf16[32,128,512]{2,1,0:T(8,128)(2,1)} %bitcast.1, f32[4096,128]{1,0:T(8,128)} %res_ref.1, f32[4096,128]{1,0:T(8,128)} %coef_ref.1), custom_call_target="tpu_custom_call" | custom-call | tf_op jit(solution)/shard_map/updates/pallas_call | solution.py:576
  76.2 0.0 copy-done
  76.2 0.0 copy-done.1
  76.2 0.0 copy-done.2
  76.2 0.0 copy-done.3
  76.2 4.5 %final.1 = (f32[4096,128]{1,0:T(8,128)}, f32[4096,128]{1,0:T(8,128)}) custom-call(s32[2]{0:T(128)S(1)} %copy-done.3, s32[2,4]{1,0:T(2,128)S(1)} %copy-done.2, f32[2,128,512]{2,1,0:T(8,128)S(1)} %get-tuple-element.5.update_ref, bf16[128,1024]{1,0:T(8,128)(2,1)S(1)} %get-tuple-element.6.low_ref, bf16[1024,4096]{1,0:T(8,128)(2,1)S(1)} %get-tuple-element.7.slab_ref, ...), custom_call_target="tpu_custom_call" | custom-call | tf_op jit(solution)/shard_map/final/pallas_call | solution.py:638
Async XLA Ops:
  0.6 75.6 %copy-start = (f32[4096,128]{1,0:T(8,128)S(1)}, f32[4096,128]{1,0:T(8,128)}, u32[]{:S(2)}) copy-start(f32[4096,128]{1,0:T(8,128)} %res_ref.1) | copy-start | bytes 6291460
  0.6 75.6 %copy-start.1 = (f32[4096,128]{1,0:T(8,128)S(1)}, f32[4096,128]{1,0:T(8,128)}, u32[]{:S(2)}) copy-start(f32[4096,128]{1,0:T(8,128)} %coef_ref.1) | copy-start | bytes 6291460
  0.7 75.6 %copy-start.2 = (s32[2,4]{1,0:T(2,128)S(1)}, s32[2,4]{1,0:T(2,128)}, u32[]{:S(2)}) copy-start(s32[2,4]{1,0:T(2,128)} %tiles_ref.3) | copy-start | bytes 100
  0.7 75.6 %copy-start.3 = (s32[2]{0:T(128)S(1)}, s32[2]{0:T(128)}, u32[]{:S(2)}) copy-start(s32[2]{0:T(128)} %owner_ref.3) | copy-start | bytes 28

commit v6 on v5

--- a/solution.py
+++ b/solution.py
@@ -197,15 +197,19 @@
         for i in reversed(range(self.first.size)):
             self.f_copy(i, 1 - self.core).wait_recv()
 
-    def drain(self):
+    def drain_scatter(self):
         for i in range(self.first.size):
             self.a_copy(i).wait_send()
-            self.f_copy(i, self.core).wait_send()
         for i in range(self.last):
             self.b_copy(i).wait_send()
-            self.e_copy(i, self.chunk).wait_send()
         for i in range(len(self.second.steps)):
             self.c_copy(i, self.slot).wait_send()
+
+    def drain_gather(self):
+        for i in range(self.last):
+            self.e_copy(i, self.chunk).wait_send()
+        for i in range(self.first.size):
+            self.f_copy(i, self.core).wait_send()
 
 
 def flow_scratch(first, second, shape, dtype):
@@ -261,9 +265,13 @@
         for flow in self.flows:
             flow.finish()
 
-    def drain(self):
+    def drain_scatter(self):
         for flow in self.flows:
-            flow.drain()
+            flow.drain_scatter()
+
+    def drain_gather(self):
+        for flow in self.flows:
+            flow.drain_gather()
 
 
 PANEL = 16
@@ -353,11 +361,12 @@
     update_ref,
     low_ref,
     slab_ref,
-    feat_ref,
     res_ref,
     coef_ref,
+    feat_ref,
     weighted_ref,
     along_ref,
+    feat_sem,
     load_sem,
     masked,
     blocks,
@@ -373,20 +382,24 @@
     swap_sem,
     *scratch,
 ):
+    def load_feat(i):
+        at = pl.ds(i * CHUNK_TILES, CHUNK_TILES)
+        return pltpu.make_async_copy(feat_hbm.at[at], feat_ref.at[at], feat_sem.at[i])
+
+    for i in range(CHUNKS):
+        load_feat(i).start()
     loads = [
         pltpu.make_async_copy(source, target, load_sem.at[i])
-        for i, (source, target) in enumerate(
-            [(feat_hbm, feat_ref), (res_hbm, res_ref), (coef_hbm, coef_ref)]
-        )
+        for i, (source, target) in enumerate([(res_hbm, res_ref), (coef_hbm, coef_ref)])
     ]
-    loads[0].start()
     chip, core = place()
     greet(chip, core)
-    for load in loads[1:]:
+    for load in loads:
         load.start()
 
     me = lax.axis_index("rows") * lax.axis_size("sub") + lax.axis_index("sub")
-    loads[0].wait()
+    for i in range(CHUNKS):
+        load_feat(i).wait()
     per_tile = TILE // FETCH_ROWS
 
     def build(s):
@@ -426,7 +439,7 @@
 
     lax.fori_loop(0, CHUNKS, norms_of, 0)
     fetch.b_to_c()
-    for load in loads[1:]:
+    for load in loads:
         load.wait()
     weighted_ref[...] = (res_ref[...] - RIDGE * coef_ref[...]).astype(BF16)
     fetch.c_to_e()
@@ -500,6 +513,8 @@
 
     inv[core] = block_kernel(core, core) + ridge
     between[...] = block_kernel(0, 1).astype(BF16)
+    fetch.drain_scatter()
+    fetch.drain_gather()
 
     def spread(k, tile):
         at = pl.ds(pl.multiple_of(k * TILE, TILE), TILE)
@@ -540,16 +555,18 @@
     split(core)
     swap(1 - core).wait_recv()
     split(1 - core)
+    sums.drain_scatter()
     sums.e_to_f()
-    sums.finish()
+    sums.flows[1].finish()
 
     both = [[thirds[s, i] for i in range(3)] for s in range(STEPS)]
     grads = jnp.transpose(grad_sum[...].reshape(BLOCK, STEPS * TARGETS))
     first = product(split3(grads[:TARGETS]), both[0]) * step_size
     first_low = first.astype(BF16)
+    past = sum(stacked_dot(split3(first), between[...]))
+    sums.flows[0].finish()
     slab_product = product_sum[...].reshape(BLOCK, BLOCK)
     shift = sum(dot(first_low, third) for third in split3(slab_product))
-    past = sum(stacked_dot(split3(first), between[...]))
     gradient = grads[TARGETS:] - shift - RIDGE * past
     second = product(split3(gradient), both[1]) * step_size
     for s, update in enumerate((first, second)):
@@ -557,8 +574,7 @@
         low_ref[:, s * BLOCK : (s + 1) * BLOCK] = update.astype(BF16)
 
     swap(core).wait_send()
-    fetch.drain()
-    sums.drain()
+    sums.drain_gather()
 
 
 def updates_of(step_size, block_owner, block_tiles, features, residual, coefficients):
@@ -579,16 +595,17 @@
             pltpu.VMEM((STEPS, TARGETS, BLOCK), F32),
             pltpu.VMEM((TARGETS, STEPS * BLOCK), BF16),
             pltpu.VMEM(slab_shape, BF16),
+            pltpu.VMEM(residual.shape, F32),
+            pltpu.VMEM(coefficients.shape, F32),
         ),
         in_specs=[smem(), smem(), hbm, hbm, hbm],
-        out_specs=(vmem(), vmem(), vmem()),
+        out_specs=(vmem(),) * 5,
         scratch_shapes=[
             pltpu.VMEM(tiled.shape, BF16),
-            pltpu.VMEM(residual.shape, F32),
-            pltpu.VMEM(coefficients.shape, F32),
             pltpu.VMEM(residual.shape, BF16),
             pltpu.VMEM((CHUNKS, 8, CHUNK), F32),
-            pltpu.SemaphoreType.DMA((3,)),
+            pltpu.SemaphoreType.DMA((CHUNKS,)),
+            pltpu.SemaphoreType.DMA((2,)),
             pltpu.VMEM(fetch_shape, BF16),
             pltpu.VMEM(fetch_shape, BF16),
             pltpu.VMEM((STEPS, BLOCK, 128), F32),
@@ -610,40 +627,65 @@
     )(block_owner, block_tiles, tiled, residual, coefficients)
 
 
-ROWS_STEP = CHUNK
+ROWS_STEP = 512
 
 
 def final_kernel(
-    owner_ref, tiles_ref, update_ref, low_ref, slab_ref, res_ref, coef_ref, res_out, coef_out
+    owner_ref,
+    tiles_ref,
+    update_ref,
+    low_ref,
+    slab_ref,
+    res_ref,
+    coef_ref,
+    res_hbm,
+    coef_hbm,
+    res_new,
+    coef_new,
+    res_sem,
+    coef_sem,
 ):
-    step = pl.program_id(0)
-    here = pl.ds(pl.multiple_of(step * ROWS_STEP, ROWS_STEP), ROWS_STEP)
-    res_out[...] = res_ref[here, :] - jnp.transpose(dot(low_ref[...], slab_ref[:, here]))
-    coef_out[...] = coef_ref[here, :]
     me = lax.axis_index("rows") * lax.axis_size("sub") + lax.axis_index("sub")
-    tiles_here = ROWS_STEP // TILE
+    coef_new[...] = coef_ref[...]
     for s in range(STEPS):
-        for t in range(BLOCK // TILE):
-            tile = tiles_ref[s, t]
-
-            @pl.when((owner_ref[s] == me) & (lax.div(tile, tiles_here) == step))
-            def _():
-                at = pl.ds(pl.multiple_of(lax.rem(tile, tiles_here) * TILE, TILE), TILE)
-                coef_out[at, :] += jnp.transpose(update_ref[s, :, t * TILE : (t + 1) * TILE])
+
+        @pl.when(owner_ref[s] == me)
+        def _():
+            for t in range(BLOCK // TILE):
+                at = pl.ds(pl.multiple_of(tiles_ref[s, t] * TILE, TILE), TILE)
+                coef_new[at, :] += jnp.transpose(update_ref[s, :, t * TILE : (t + 1) * TILE])
+
+    coef_copy = pltpu.make_async_copy(coef_new, coef_hbm, coef_sem)
+    coef_copy.start()
+    copies = []
+    for i in range(res_ref.shape[0] // ROWS_STEP):
+        here = pl.ds(i * ROWS_STEP, ROWS_STEP)
+        res_new[here, :] = res_ref[here, :] - jnp.transpose(dot(low_ref[...], slab_ref[:, here]))
+        copies.append(
+            pltpu.make_async_copy(res_new.at[here, :], res_hbm.at[here, :], res_sem.at[i])
+        )
+        copies[-1].start()
+    for copy in copies + [coef_copy]:
+        copy.wait()
 
 
 def final(owner, tiles, updates, low, slabs, residual, coefficients):
     rows = residual.shape[0]
-    chunk = pl.BlockSpec((ROWS_STEP, TARGETS), lambda i: (i, 0))
+    anywhere = pl.BlockSpec(memory_space=pl.ANY)
     return pl.pallas_call(
         final_kernel,
-        grid=(rows // ROWS_STEP,),
         out_shape=(
             jax.ShapeDtypeStruct(residual.shape, F32),
             jax.ShapeDtypeStruct(coefficients.shape, F32),
         ),
         in_specs=[smem(), smem(), vmem(), vmem(), vmem(), vmem(), vmem()],
-        out_specs=(chunk, chunk),
+        out_specs=(anywhere, anywhere),
+        scratch_shapes=[
+            pltpu.VMEM(residual.shape, F32),
+            pltpu.VMEM(coefficients.shape, F32),
+            pltpu.SemaphoreType.DMA((rows // ROWS_STEP,)),
+            pltpu.SemaphoreType.DMA,
+        ],
         compiler_params=pltpu.CompilerParams(vmem_limit_bytes=24 << 20),
         name="final",
     )(owner, tiles, updates, low, slabs, residual, coefficients)
@@ -652,10 +694,10 @@
 def local(features, residual, coefficients, block_owner, block_tiles):
     devices = lax.axis_size("rows") * lax.axis_size("sub")
     step_size = 1.0 / math.sqrt(features.shape[0] * devices)
-    updates, low, slabs = updates_of(
+    results = updates_of(
         step_size, block_owner, block_tiles, features, residual, coefficients
     )
-    return final(block_owner, block_tiles, updates, low, slabs, residual, coefficients)
+    return final(block_owner, block_tiles, *results)
 
 
 def solution(mesh):

time: 80.8 us -> 79.9 us (0.989)
  Pallas kernels: 80 us -> 79 us
    pallas_call x1, Pallas kernels: 4.47 us -> 3.27 us  [final(): pl.pallas_call(final_kernel, out_shape=(jax.ShapeDtypeStruct(residual.sha...]
where the time goes in v6:
time: 79.9 us; the launch traced here: 79.8 us
  Pallas kernels  79 us (99%)
  between operations  0.83 us (1%)
    pallas_call x1, Pallas kernels, updates_of(): pl.pallas_call(functools.partial(update_kernel, step_size), out_shape=(pl...  75.7 us
    pallas_call x1, Pallas kernels, final(): pl.pallas_call(final_kernel, out_shape=(jax.ShapeDtypeStruct(residual.sha...  3.27 us

profile of v6, /device:TPU:1, one launch (start us, length us, event | category | flops | bytes accessed | tf_op | source)
XLA Modules:
  0.0 79.8 jit_solution(2360198243568670615)
XLA Ops:
  0.6 0.0 copy-start
  0.6 0.0 copy-start.1
  0.7 75.7 %updates.1 = (f32[2,128,512]{2,1,0:T(8,128)S(1)}, bf16[128,1024]{1,0:T(8,128)(2,1)S(1)}, bf16[1024,4096]{1,0:T(8,128)(2,1)S(1)}, f32[4096,128]{1,0:T(8,128)S(1)}, f32[4096,128]{1,0:T(8,128)S(1)}) custom-call(s32[2]{0:T(128)} %owner_ref.3, s32[2,4]{1,0:T(2,128)} %tiles_ref.3, bf16[32,128,512]{2,1,0:T(8,128)(2,1)} %bitcast.1, f32[4096,128]{1,0:T(8,128)} %res_hbm.1, ...), custom_call_target="tpu_custom_call" | custom-call | tf_op jit(solution)/shard_map/updates/pallas_call | solution.py:592
  76.4 0.0 copy-done
  76.4 0.0 copy-done.1
  76.4 3.3 %final.1 = (f32[4096,128]{1,0:T(8,128)}, f32[4096,128]{1,0:T(8,128)}) custom-call(s32[2]{0:T(128)S(1)} %copy-done.1, s32[2,4]{1,0:T(2,128)S(1)} %copy-done, f32[2,128,512]{2,1,0:T(8,128)S(1)} %get-tuple-element.7.update_ref, bf16[128,1024]{1,0:T(8,128)(2,1)S(1)} %get-tuple-element.8.low_ref, bf16[1024,4096]{1,0:T(8,128)(2,1)S(1)} %get-tuple-element.9.slab_ref, ...), custom_call_target="tpu_custom_call" | custom-call | tf_op jit(solution)/shard_map/final/pallas_call | solution.py:675
Async XLA Ops:
  0.6 75.8 %copy-start = (s32[2,4]{1,0:T(2,128)S(1)}, s32[2,4]{1,0:T(2,128)}, u32[]{:S(2)}) copy-start(s32[2,4]{1,0:T(2,128)} %tiles_ref.3) | copy-start | bytes 100
  0.6 75.8 %copy-start.1 = (s32[2]{0:T(128)S(1)}, s32[2]{0:T(128)}, u32[]{:S(2)}) copy-start(s32[2]{0:T(128)} %owner_ref.3) | copy-start | bytes 28

commit v7 on v6

--- a/solution.py
+++ b/solution.py
@@ -9,7 +9,6 @@
 from jax.sharding import PartitionSpec as P
 
 MESH = pl.DeviceIdType.MESH
-HI = lax.Precision.HIGHEST
 F32 = jnp.float32
 BF16 = jnp.bfloat16
 
@@ -278,14 +277,34 @@
 PANELS = TILE // PANEL
 
 
+def split3(wide):
+    high = wide.astype(BF16)
+    rest = wide - high.astype(F32)
+    middle = rest.astype(BF16)
+    low = (rest - middle.astype(F32)).astype(BF16)
+    return high, middle, low
+
+
+LEFT_THIRDS = (0, 0, 1, 0, 2, 1)
+RIGHT_THIRDS = (0, 1, 0, 2, 0, 1)
+
+
+def wide_dot(left, right):
+    left, right = split3(left), split3(right)
+    return dot(
+        jnp.concatenate([left[i] for i in LEFT_THIRDS], axis=1),
+        jnp.concatenate([right[i] for i in RIGHT_THIRDS], axis=0),
+    )
+
+
 def eliminate(a, panel):
     n, first = TILE, panel * PANEL
     mine = slice(first, first + PANEL)
     row = lax.broadcasted_iota(jnp.int32, (PANEL, n), 0)
     lane = lax.broadcasted_iota(jnp.int32, (PANEL, n), 1)
-    lane_all = lax.broadcasted_iota(jnp.int32, (n, n), 1)
-    columns = [jnp.broadcast_to(a[:, first + j : first + j + 1], (n, n)) for j in range(PANEL)]
-    square = [column[mine] for column in columns]
+    square = [
+        jnp.broadcast_to(a[mine, first + j : first + j + 1], (PANEL, n)) for j in range(PANEL)
+    ]
     rows = jnp.where(
         (lane >= first) & (lane < first + PANEL),
         jnp.where(lane - first == row, 1.0, 0.0),
@@ -297,20 +316,22 @@
         for j in range(k + 1, PANEL):
             square[j] = square[j] - column * (square[j][k : k + 1] * inverse)
         rows = rows - column * (rows[k : k + 1] * inverse)
-    change = columns[0] * rows[0:1]
-    for j in range(1, PANEL):
-        change = change + columns[j] * rows[j : j + 1]
-    a = jnp.where((lane_all >= first) & (lane_all < first + PANEL), 0.0, a) - change
+    lane_all = lax.broadcasted_iota(jnp.int32, (n, n), 1)
+    inside = (lane_all >= first) & (lane_all < first + PANEL)
+    columns = jnp.where(inside, a, 0.0)
+    if first:
+        columns = pltpu.roll(columns, n - first, 1)
+    left = [third.astype(F32) for third in split3(columns)]
+    right = split3(rows)
+    packed = left[0]
+    for i, t in enumerate(LEFT_THIRDS[1:]):
+        packed = packed + pltpu.roll(left[t], PANEL * (i + 1), 1)
+    below = [right[t] for t in RIGHT_THIRDS]
+    below.append(jnp.zeros((n - PANEL * len(below), n), BF16))
+    change = dot(packed.astype(BF16), jnp.concatenate(below, axis=0))
+    a = jnp.where(inside, 0.0, a) - change
     pieces = [a[:first], rows, a[first + PANEL :]]
     return jnp.concatenate([piece for piece in pieces if piece.shape[0]], axis=0)
-
-
-def split3(wide):
-    high = wide.astype(BF16)
-    rest = wide - high.astype(F32)
-    middle = rest.astype(BF16)
-    low = (rest - middle.astype(F32)).astype(BF16)
-    return high, middle, low
 
 
 def stacked_dot(thirds, right):
@@ -378,7 +399,6 @@
     inv,
     thirds,
     between,
-    first_tile,
     swap_sem,
     *scratch,
 ):
@@ -460,13 +480,6 @@
         return dot_nt(block_rows(sides[unit]), feat)
 
     set_norm(core)
-    row = lax.broadcasted_iota(jnp.int32, (BLOCK, BLOCK), 0)
-    lane = lax.broadcasted_iota(jnp.int32, (BLOCK, BLOCK), 1)
-    ridge = jnp.where(row == lane, RIDGE, 0.0)
-    corner = blocks[core, 0 : TILE // FETCH_ROWS].reshape(TILE, WIDTH)
-    corner_norm = norm_ref[core, 0:TILE, 0:1]
-    tile = kernel_of(dot_nt(corner, corner), corner_norm, along_lanes(corner_norm))
-    tile = tile + ridge[:TILE, :TILE]
     cross = cross_of(0)
     for unit in range(units):
         i = unit % CHUNKS
@@ -477,10 +490,7 @@
         slab = kernel_of(cross, norm_ref[sides[unit]][:, 0:1], along_ref[i][0:1, :]).astype(BF16)
         at = pl.ds(pl.multiple_of(sides[unit] * BLOCK, BLOCK), BLOCK)
         slab_ref[at, i * CHUNK : (i + 1) * CHUNK] = slab
-        if unit < PANELS:
-            tile = eliminate(tile, unit)
         cross = later
-    first_tile[...] = tile
 
     def share(half):
         at = [pl.ds(pl.multiple_of(s * BLOCK + half * HALF, HALF), HALF) for s in range(STEPS)]
@@ -511,7 +521,9 @@
         cross = dot_nt(block_rows(a), block_rows(b))
         return kernel_of(cross, norm_ref[a][:, 0:1], along_lanes(norm_ref[b][:, 0:1]))
 
-    inv[core] = block_kernel(core, core) + ridge
+    row = lax.broadcasted_iota(jnp.int32, (BLOCK, BLOCK), 0)
+    lane = lax.broadcasted_iota(jnp.int32, (BLOCK, BLOCK), 1)
+    inv[core] = block_kernel(core, core) + jnp.where(row == lane, RIDGE, 0.0)
     between[...] = block_kernel(0, 1).astype(BF16)
     fetch.drain_scatter()
     fetch.drain_gather()
@@ -519,14 +531,19 @@
     def spread(k, tile):
         at = pl.ds(pl.multiple_of(k * TILE, TILE), TILE)
         inside = lax.div(lax.broadcasted_iota(jnp.int32, (TILE, BLOCK), 1), TILE) == k
-        lead = dot(tile, inv[core, at, :], HI)
+        lead = wide_dot(tile, inv[core, at, :])
         lead = jnp.where(inside, jnp.concatenate([tile] * (BLOCK // TILE), axis=1), lead)
         column = inv[core, :, at]
         inv[core, :, at] = jnp.zeros_like(column)
-        inv[core] -= dot(column, lead, HI)
+        inv[core] -= wide_dot(column, lead)
         inv[core, at, :] = lead
 
-    stages = {(1, 3): sums.b_to_c, (3, 0): sums.c_to_e}
+    stages = {(1, 0): sums.b_to_c, (2, 4): sums.c_to_e}
+
+    def look(k, part):
+        for (at_k, at_part), stage in stages.items():
+            if at_part == part:
+                pl.when(k == at_k)(stage)
 
     def step(k, carry):
         at = pl.ds(pl.multiple_of(k * TILE, TILE), TILE)
@@ -535,14 +552,12 @@
             for panel in range(part * PANELS // 4, (part + 1) * PANELS // 4):
                 tile = eliminate(tile, panel)
             inv[core, at, at] = tile
-            for (at_k, at_part), stage in stages.items():
-                if at_part == part:
-                    pl.when(k == at_k)(stage)
+            look(k, part)
         spread(k, inv[core, at, at])
+        look(k, 4)
         return carry
 
-    spread(0, first_tile[...])
-    lax.fori_loop(1, BLOCK // TILE, step, 0)
+    lax.fori_loop(0, BLOCK // TILE, step, 0)
 
     def swap(side):
         return remote(inv.at[core], inv.at[side], swap_sem, 0, (chip, 1 - core))
@@ -616,7 +631,6 @@
             pltpu.VMEM((STEPS, BLOCK, BLOCK), F32),
             pltpu.VMEM((STEPS, 3, BLOCK, BLOCK), BF16),
             pltpu.VMEM((BLOCK, BLOCK), BF16),
-            pltpu.VMEM((TILE, TILE), F32),
             pltpu.SemaphoreType.DMA((2, 1)),
             *flows,
         ],

time: 79.9 us -> 78.4 us (0.981)
  Pallas kernels: 79 us -> 77.5 us
    pallas_call x1, Pallas kernels: 75.7 us -> 74.2 us  [updates_of(): pl.pallas_call(functools.partial(update_kernel, step_size), out_shape=(pl...]
where the time goes in v7:
time: 78.4 us; the launch traced here: 78.3 us
  Pallas kernels  77.5 us (99%)
  between operations  0.83 us (1%)
    pallas_call x1, Pallas kernels, updates_of(): pl.pallas_call(functools.partial(update_kernel, step_size), out_shape=(pl...  74.2 us
    pallas_call x1, Pallas kernels, final(): pl.pallas_call(final_kernel, out_shape=(jax.ShapeDtypeStruct(residual.sha...  3.27 us

profile of v7, /device:TPU:1, one launch (start us, length us, event | category | flops | bytes accessed | tf_op | source)
XLA Modules:
  0.0 78.3 jit_solution(16361841934431645669)
XLA Ops:
  0.6 0.0 copy-start
  0.6 0.0 copy-start.1
  0.7 74.2 %updates.1 = (f32[2,128,512]{2,1,0:T(8,128)S(1)}, bf16[128,1024]{1,0:T(8,128)(2,1)S(1)}, bf16[1024,4096]{1,0:T(8,128)(2,1)S(1)}, f32[4096,128]{1,0:T(8,128)S(1)}, f32[4096,128]{1,0:T(8,128)S(1)}) custom-call(s32[2]{0:T(128)} %owner_ref.3, s32[2,4]{1,0:T(2,128)} %tiles_ref.3, bf16[32,128,512]{2,1,0:T(8,128)(2,1)} %bitcast.1, f32[4096,128]{1,0:T(8,128)} %res_hbm.1, ...), custom_call_target="tpu_custom_call" | custom-call | tf_op jit(solution)/shard_map/updates/pallas_call | solution.py:607
  74.9 0.0 copy-done
  74.9 0.0 copy-done.1
  74.9 3.3 %final.1 = (f32[4096,128]{1,0:T(8,128)}, f32[4096,128]{1,0:T(8,128)}) custom-call(s32[2]{0:T(128)S(1)} %copy-done.1, s32[2,4]{1,0:T(2,128)S(1)} %copy-done, f32[2,128,512]{2,1,0:T(8,128)S(1)} %get-tuple-element.7.update_ref, bf16[128,1024]{1,0:T(8,128)(2,1)S(1)} %get-tuple-element.8.low_ref, bf16[1024,4096]{1,0:T(8,128)(2,1)S(1)} %get-tuple-element.9.slab_ref, ...), custom_call_target="tpu_custom_call" | custom-call | tf_op jit(solution)/shard_map/final/pallas_call | solution.py:689
Async XLA Ops:
  0.6 74.3 %copy-start = (s32[2,4]{1,0:T(2,128)S(1)}, s32[2,4]{1,0:T(2,128)}, u32[]{:S(2)}) copy-start(s32[2,4]{1,0:T(2,128)} %tiles_ref.3) | copy-start | bytes 100
  0.6 74.3 %copy-start.1 = (s32[2]{0:T(128)S(1)}, s32[2]{0:T(128)}, u32[]{:S(2)}) copy-start(s32[2]{0:T(128)} %owner_ref.3) | copy-start | bytes 28

commit v8 on v7

--- a/solution.py
+++ b/solution.py
@@ -75,24 +75,41 @@
     return sum(min(s, size - s) for s, size in zip(step, SIZES))
 
 
+COLUMN_STEPS = sorted(
+    [(i, j, 0) for i in range(NX) for j in range(NY) if i or j], key=lambda s: -hops(s)
+)
+GROUP_STEPS = (2, 1, 3, 0)
+
+
 class Columns:
     size = NX * NY
-    steps = sorted(
-        [(i, j, 0) for i in range(NX) for j in range(NY) if i or j], key=lambda s: -hops(s)
-    )
+    steps = COLUMN_STEPS
+    groups = [[i for i, s in enumerate(COLUMN_STEPS) if s[0] == dx] for dx in GROUP_STEPS]
+    members = NY
 
     @staticmethod
     def number(chip):
         return chip[0] * NY + chip[1]
 
+    @staticmethod
+    def group_start(chip, j):
+        return moved(chip, (-GROUP_STEPS[j], 0, 0))[0] * NY
+
 
 class Planes:
     size = NZ
     steps = sorted([(0, 0, k) for k in range(1, NZ)], key=lambda s: -hops(s))
 
+    groups = [list(range(NZ - 1))]
+    members = NZ
+
     @staticmethod
     def number(chip):
         return chip[2]
+
+    @staticmethod
+    def group_start(chip, j):
+        return 0
 
 
 def greet(chip, core):
@@ -118,10 +135,26 @@
     )
 
 
+class Chunks:
+    def __init__(self, ref, per=1, lanes=None):
+        self.ref, self.per, self.lanes = ref, per, lanes
+
+    def some(self, side, index):
+        if self.lanes is None:
+            return self.ref.at[side, index]
+        return self.ref.at[side, index, :, self.lanes]
+
+    def one(self, side, chunk):
+        return self.some(side, chunk if self.per == 1 else pl.ds(self.per * chunk, self.per))
+
+    def run(self, side, start, count):
+        return self.some(side, pl.ds(self.per * start, self.per * count))
+
+
 class Flow:
-    def __init__(self, chip, core, first, second, part_at, total_at, scratch):
+    def __init__(self, chip, core, first, second, part, total, scratch):
         self.chip, self.core, self.first, self.second = chip, core, first, second
-        self.part_at, self.total_at = part_at, total_at
+        self.part, self.total = part, total
         self.recv_a, self.half, self.recv_b, self.recv_c = scratch[:4]
         self.sem_a, self.sem_b, self.sem_c, self.sem_e, self.sem_f = scratch[4:]
         self.steps = first.steps + [(0, 0, 0)]
@@ -137,9 +170,9 @@
     def behind(self, i):
         return self.first.number(moved(self.chip, back(self.steps[i])))
 
-    def a_copy(self, i):
-        part = self.part_at(1 - self.core, self.ahead(i)[1])
-        return remote(part, self.recv_a.at[i], self.sem_a, i, self.mate)
+    def a_copy(self):
+        part = self.part.run(1 - self.core, 0, self.first.size)
+        return remote(part, self.recv_a.at[0], self.sem_a, 0, self.mate)
 
     def b_copy(self, i):
         return remote(self.half.at[i], self.recv_b.at[i], self.sem_b, i, self.ahead(i)[0])
@@ -150,20 +183,20 @@
         return remote(mine, target, self.sem_c, i, (there, self.core))
 
     def e_copy(self, i, chunk):
-        mine, target = self.total_at(self.core, self.chunk), self.total_at(self.core, chunk)
+        mine, target = self.total.one(self.core, self.chunk), self.total.one(self.core, chunk)
         return remote(mine, target, self.sem_e, i, self.ahead(i)[0])
 
-    def f_copy(self, i, side):
-        chunk = self.behind(i)
-        mine, target = self.total_at(self.core, chunk), self.total_at(side, chunk)
-        return remote(mine, target, self.sem_f, i, self.mate)
-
-    def start_a(self, i):
-        self.a_copy(i).start()
+    def f_copy(self, j, side):
+        start, count = self.first.group_start(self.chip, j), self.first.members
+        mine, target = self.total.run(self.core, start, count), self.total.run(side, start, count)
+        return remote(mine, target, self.sem_f, j, self.mate)
 
     def a_to_b(self, i):
-        self.a_copy(i).wait_recv()
-        self.half[i] = self.part_at(self.core, self.ahead(i)[1])[...] + self.recv_a[i]
+        if i == 0:
+            self.a_copy().wait_recv()
+        chunk = self.ahead(i)[1]
+        other = Chunks(self.recv_a, self.part.per).one(0, chunk)
+        self.half[i] = self.part.one(self.core, chunk)[...] + other[...]
         if i < self.last:
             self.b_copy(i).start()
 
@@ -183,22 +216,21 @@
         chunk = self.recv_c[0]
         for i in range(1, self.second.size):
             chunk = chunk + self.recv_c[i]
-        self.total_at(self.core, self.chunk)[...] = chunk
+        self.total.one(self.core, self.chunk)[...] = chunk
         for i in range(self.last):
             self.e_copy(i, self.chunk).start()
-        self.f_copy(self.last, self.core).start()
-
-    def e_to_f(self, i):
-        self.e_copy(i, self.behind(i)).wait_recv()
-        self.f_copy(i, self.core).start()
+
+    def e_to_f(self, j):
+        for i in self.first.groups[j]:
+            self.e_copy(i, self.behind(i)).wait_recv()
+        self.f_copy(j, self.core).start()
 
     def finish(self):
-        for i in reversed(range(self.first.size)):
-            self.f_copy(i, 1 - self.core).wait_recv()
+        for j in range(len(self.first.groups)):
+            self.f_copy(j, 1 - self.core).wait_recv()
 
     def drain_scatter(self):
-        for i in range(self.first.size):
-            self.a_copy(i).wait_send()
+        self.a_copy().wait_send()
         for i in range(self.last):
             self.b_copy(i).wait_send()
         for i in range(len(self.second.steps)):
@@ -207,25 +239,25 @@
     def drain_gather(self):
         for i in range(self.last):
             self.e_copy(i, self.chunk).wait_send()
-        for i in range(self.first.size):
-            self.f_copy(i, self.core).wait_send()
-
-
-def flow_scratch(first, second, shape, dtype):
+        for j in range(len(self.first.groups)):
+            self.f_copy(j, self.core).wait_send()
+
+
+def flow_scratch(first, second, half, shape, dtype):
     def pair(n):
         return pltpu.SemaphoreType.DMA((2, n))
 
     n1, n2 = len(first.steps), len(second.steps)
     return [
-        pltpu.VMEM((first.size, *shape), dtype),
+        pltpu.VMEM((1, *half), dtype),
         pltpu.VMEM((first.size, *shape), dtype),
         pltpu.VMEM((n1, *shape), dtype),
         pltpu.VMEM((second.size, *shape), dtype),
-        pair(first.size),
+        pair(1),
         pair(n1),
         pair(n2),
         pair(n1),
-        pair(first.size),
+        pair(len(first.groups)),
     ]
 
 
@@ -244,7 +276,8 @@
                     call(flow, i)
 
     def start_a(self):
-        self.in_turn(lambda f: f.first.size, lambda f, i: f.start_a(i))
+        for flow in self.flows:
+            flow.a_copy().start()
 
     def a_to_b(self):
         self.in_turn(lambda f: f.first.size, lambda f, i: f.a_to_b(i))
@@ -258,7 +291,7 @@
             flow.c_to_e()
 
     def e_to_f(self):
-        self.in_turn(lambda f: f.last, lambda f, i: f.e_to_f(f.last - 1 - i))
+        self.in_turn(lambda f: len(f.first.groups), lambda f, j: f.e_to_f(j))
 
     def finish(self):
         for flow in self.flows:
@@ -365,9 +398,16 @@
 
 FETCH_ROWS = BLOCK // NQ
 FETCH_CUT = 384
-FETCH_FLOWS = ((Columns, Planes, (FETCH_ROWS, FETCH_CUT)), (Planes, Columns, (2, FETCH_ROWS, WIDTH - FETCH_CUT)))
+FETCH_REST = WIDTH - FETCH_CUT
 HALF = BLOCK // 2
-SUM_FLOWS = ((Columns, Planes, (HALF // NQ, BLOCK)), (Planes, Columns, (HALF // NZ, STEPS * TARGETS)))
+FETCH_FLOWS = (
+    (Columns, Planes, (NQ, FETCH_ROWS, FETCH_CUT), (FETCH_ROWS, FETCH_CUT)),
+    (Planes, Columns, (NQ, FETCH_ROWS, FETCH_REST), (NQ // NZ, FETCH_ROWS, FETCH_REST)),
+)
+SUM_FLOWS = (
+    (Columns, Planes, (NQ, HALF // NQ, BLOCK), (HALF // NQ, BLOCK)),
+    (Planes, Columns, (NZ, HALF // NZ, STEPS * TARGETS), (HALF // NZ, STEPS * TARGETS)),
+)
 CHUNKS = ROWS_DEV // CHUNK
 CHUNK_TILES = CHUNK // TILE
 
@@ -430,17 +470,15 @@
                 at = slice(i * FETCH_ROWS, (i + 1) * FETCH_ROWS)
                 masked[s, t * per_tile + i] = tile[at] * mine
 
-    left, right = pl.ds(0, FETCH_CUT), pl.ds(FETCH_CUT, WIDTH - FETCH_CUT)
-
     def pair_of(ref):
         return (
-            lambda side, chunk: ref.at[side, chunk, :, left],
-            lambda side, chunk: ref.at[side, pl.ds(2 * chunk, 2), :, right],
+            Chunks(ref, 1, pl.ds(0, FETCH_CUT)),
+            Chunks(ref, NQ // NZ, pl.ds(FETCH_CUT, FETCH_REST)),
         )
 
     def flows_of(kinds, parts, totals, scratch):
         flows = []
-        for i, (first, second, _) in enumerate(kinds):
+        for i, (first, second, _, _) in enumerate(kinds):
             mine = scratch[i * FLOW_SCRATCH : (i + 1) * FLOW_SCRATCH]
             flows.append(Flow(chip, core, first, second, parts[i], totals[i], mine))
         return Flows(*flows)
@@ -502,14 +540,8 @@
 
     sums = flows_of(
         SUM_FLOWS,
-        (
-            lambda side, chunk: product_part.at[side, chunk],
-            lambda side, chunk: grad_part.at[side, chunk],
-        ),
-        (
-            lambda side, chunk: product_sum.at[side, chunk],
-            lambda side, chunk: grad_sum.at[side, chunk],
-        ),
+        (Chunks(product_part), Chunks(grad_part)),
+        (Chunks(product_sum), Chunks(grad_sum)),
         scratch[2 * FLOW_SCRATCH :],
     )
     share(1 - core)
@@ -600,10 +632,10 @@
     product_shape = (2, NQ, HALF // NQ, BLOCK)
     grad_shape = (2, NZ, HALF // NZ, STEPS * TARGETS)
     flows = []
-    for first, second, shape in FETCH_FLOWS:
-        flows += flow_scratch(first, second, shape, BF16)
-    for first, second, shape in SUM_FLOWS:
-        flows += flow_scratch(first, second, shape, F32)
+    for kind in FETCH_FLOWS:
+        flows += flow_scratch(*kind, BF16)
+    for kind in SUM_FLOWS:
+        flows += flow_scratch(*kind, F32)
     return pl.pallas_call(
         functools.partial(update_kernel, step_size),
         out_shape=(

time: 78.4 us -> 77.9 us (level)
  no operation moved by 1% of the time
where the time goes in v8:
time: 77.9 us; the launch traced here: 77.8 us
  Pallas kernels  76.9 us (99%)
  between operations  0.83 us (1%)
    pallas_call x1, Pallas kernels, updates_of(): pl.pallas_call(functools.partial(update_kernel, step_size), out_shape=(pl...  73.7 us
    pallas_call x1, Pallas kernels, final(): pl.pallas_call(final_kernel, out_shape=(jax.ShapeDtypeStruct(residual.sha...  3.26 us

profile of v8, /device:TPU:1, one launch (start us, length us, event | category | flops | bytes accessed | tf_op | source)
XLA Modules:
  0.0 77.8 jit_solution(15968510531922264752)
XLA Ops:
  0.6 0.0 copy-start
  0.6 0.0 copy-start.1
  0.7 73.7 %updates.1 = (f32[2,128,512]{2,1,0:T(8,128)S(1)}, bf16[128,1024]{1,0:T(8,128)(2,1)S(1)}, bf16[1024,4096]{1,0:T(8,128)(2,1)S(1)}, f32[4096,128]{1,0:T(8,128)S(1)}, f32[4096,128]{1,0:T(8,128)S(1)}) custom-call(s32[2]{0:T(128)} %owner_ref.3, s32[2,4]{1,0:T(2,128)} %tiles_ref.3, bf16[32,128,512]{2,1,0:T(8,128)(2,1)} %bitcast.1, f32[4096,128]{1,0:T(8,128)} %res_hbm.1, ...), custom_call_target="tpu_custom_call" | custom-call | tf_op jit(solution)/shard_map/updates/pallas_call | solution.py:639
  74.3 0.0 copy-done
  74.3 0.0 copy-done.1
  74.3 3.3 %final.1 = (f32[4096,128]{1,0:T(8,128)}, f32[4096,128]{1,0:T(8,128)}) custom-call(s32[2]{0:T(128)S(1)} %copy-done.1, s32[2,4]{1,0:T(2,128)S(1)} %copy-done, f32[2,128,512]{2,1,0:T(8,128)S(1)} %get-tuple-element.7.update_ref, bf16[128,1024]{1,0:T(8,128)(2,1)S(1)} %get-tuple-element.8.low_ref, bf16[1024,4096]{1,0:T(8,128)(2,1)S(1)} %get-tuple-element.9.slab_ref, ...), custom_call_target="tpu_custom_call" | custom-call | tf_op jit(solution)/shard_map/final/pallas_call | solution.py:721
Async XLA Ops:
  0.6 73.7 %copy-start = (s32[2,4]{1,0:T(2,128)S(1)}, s32[2,4]{1,0:T(2,128)}, u32[]{:S(2)}) copy-start(s32[2,4]{1,0:T(2,128)} %tiles_ref.3) | copy-start | bytes 100
  0.6 73.7 %copy-start.1 = (s32[2]{0:T(128)S(1)}, s32[2]{0:T(128)}, u32[]{:S(2)}) copy-start(s32[2]{0:T(128)} %owner_ref.3) | copy-start | bytes 28

commit v9 on v8

--- a/solution.py
+++ b/solution.py
@@ -692,7 +692,16 @@
     coef_sem,
 ):
     me = lax.axis_index("rows") * lax.axis_size("sub") + lax.axis_index("sub")
-    coef_new[...] = coef_ref[...]
+    owns = (owner_ref[0] == me) | (owner_ref[1] == me)
+
+    @pl.when(jnp.logical_not(owns))
+    def _():
+        pltpu.make_async_copy(coef_ref, coef_hbm, coef_sem).start()
+
+    @pl.when(owns)
+    def _():
+        coef_new[...] = coef_ref[...]
+
     for s in range(STEPS):
 
         @pl.when(owner_ref[s] == me)
@@ -702,7 +711,11 @@
                 coef_new[at, :] += jnp.transpose(update_ref[s, :, t * TILE : (t + 1) * TILE])
 
     coef_copy = pltpu.make_async_copy(coef_new, coef_hbm, coef_sem)
-    coef_copy.start()
+
+    @pl.when(owns)
+    def _():
+        coef_copy.start()
+
     copies = []
     for i in range(res_ref.shape[0] // ROWS_STEP):
         here = pl.ds(i * ROWS_STEP, ROWS_STEP)

time: 77.9 us -> 78 us (level)
  no operation moved by 1% of the time
where the time goes in v9:
time: 78 us; the launch traced here: 78.3 us
  Pallas kernels  77.5 us (99%)
  between operations  0.83 us (1%)
    pallas_call x1, Pallas kernels, updates_of(): pl.pallas_call(functools.partial(update_kernel, step_size), out_shape=(pl...  73.7 us
    pallas_call x1, Pallas kernels, final(): pl.pallas_call(final_kernel, out_shape=(jax.ShapeDtypeStruct(residual.sha...  3.81 us

profile of v9, /device:TPU:1, one launch (start us, length us, event | category | flops | bytes accessed | tf_op | source)
XLA Modules:
  0.0 78.3 jit_solution(8948521130791766162)
XLA Ops:
  0.6 0.0 copy-start
  0.6 0.0 copy-start.1
  0.7 73.7 %updates.1 = (f32[2,128,512]{2,1,0:T(8,128)S(1)}, bf16[128,1024]{1,0:T(8,128)(2,1)S(1)}, bf16[1024,4096]{1,0:T(8,128)(2,1)S(1)}, f32[4096,128]{1,0:T(8,128)S(1)}, f32[4096,128]{1,0:T(8,128)S(1)}) custom-call(s32[2]{0:T(128)} %owner_ref.3, s32[2,4]{1,0:T(2,128)} %tiles_ref.3, bf16[32,128,512]{2,1,0:T(8,128)(2,1)} %bitcast.1, f32[4096,128]{1,0:T(8,128)} %res_hbm.1, ...), custom_call_target="tpu_custom_call" | custom-call | tf_op jit(solution)/shard_map/updates/pallas_call | solution.py:639
  74.3 0.0 copy-done
  74.3 0.0 copy-done.1
  74.3 3.8 %final.1 = (f32[4096,128]{1,0:T(8,128)}, f32[4096,128]{1,0:T(8,128)}) custom-call(s32[2]{0:T(128)S(1)} %copy-done.1, s32[2,4]{1,0:T(2,128)S(1)} %copy-done, f32[2,128,512]{2,1,0:T(8,128)S(1)} %get-tuple-element.7.update_ref, bf16[128,1024]{1,0:T(8,128)(2,1)S(1)} %get-tuple-element.8.low_ref, bf16[1024,4096]{1,0:T(8,128)(2,1)S(1)} %get-tuple-element.9.slab_ref, ...), custom_call_target="tpu_custom_call" | custom-call | tf_op jit(solution)/shard_map/final/pallas_call | solution.py:734
Async XLA Ops:
  0.6 73.7 %copy-start = (s32[2,4]{1,0:T(2,128)S(1)}, s32[2,4]{1,0:T(2,128)}, u32[]{:S(2)}) copy-start(s32[2,4]{1,0:T(2,128)} %tiles_ref.3) | copy-start | bytes 100
  0.6 73.7 %copy-start.1 = (s32[2]{0:T(128)S(1)}, s32[2]{0:T(128)}, u32[]{:S(2)}) copy-start(s32[2]{0:T(128)} %owner_ref.3) | copy-start | bytes 28
